TPU v7x, 32 devices: a whole 2x2x4 slice. The times are simulated.
32 devices in a mesh: groups: 2 (over x), clus: 16 (over z, y, core).
Axes of the slice: x: 2, y: 2, z: 4, core: 2. Of those that a mesh axis runs over, the one named last changes fastest.
Arguments:
- point_offsets: float32 [512, 3, 128], P(('groups', 'clus')), parts along dimension 0, may hold values from -0.3 to 0.3
- panel_normals: float32 [512, 3, 128], P(('groups', 'clus')), parts along dimension 0, may hold values from -0.5 to 0.5
- right_sketch: float32 [512, 64, 128], P(('groups', 'clus')), parts along dimension 0, may hold values from -6 to 6
- left_sketch: float32 [512, 64, 128], P(('groups', 'clus')), parts along dimension 0, may hold values from -6 to 6
- pair_count: int32 [32], P(('groups', 'clus')), parts along dimension 0, may hold values from 1 to 128, 1536 in all
- pair_rows: int32 [4096], P(('groups', 'clus')), parts along dimension 0, may hold values from 0 to 15
- pair_offset: int32 [4096, 1], P(('groups', 'clus')), parts along dimension 0, may hold values from 0 to 14; in each aligned block of 128 rows (0 to 127, 128 to 255, ...) at most 16 rows name the same one
- pair_cols: int32 [4096], P(('groups', 'clus')), parts along dimension 0, may hold values from 0 to 15, as said below
Outputs:
- row_sketch: float32 [512, 64, 128], P(('groups', 'clus')), parts along dimension 0
- col_sketch: float32 [512, 64, 128], P(('groups', 'clus')), parts along dimension 0
There are 2 independent parts, one for each index of `groups`. A program takes and returns all parts, laid end to end along the dimension named above; each array names one. Nothing has to cross between parts.
Inputs may be any that keep to these rules, and one draw needn't show every extreme that they name: `pair_offset`: among the 128 slots of any one device no value appears more than 16 times; on some devices one value appears exactly 16 times. `pair_cols`: for every slot the first lattice coordinates of the centers of its row and column clusters differ by 2 or more (the pair is admissible).
All inputs are finite; a program needn't handle non-finite values. No bound on the sum of `pair_count` on one device may be relied on, other than what follows from the above.
Results may differ from a plain program's by a relative error of at most 0.0003.
Values sent between devices are 32-bit elements; how exact they have to be, the bound alone decides.
A program may use at most 64 MiB of HBM per device.

v0:
```python
import math

import jax
import jax.numpy as jnp
from jax import lax
from jax.sharding import PartitionSpec as P

wave_number = 8.0
precise = lax.Precision.HIGHEST


def centers_of(cluster_ids):
    return jnp.stack([cluster_ids % 16, cluster_ids // 16 % 8, cluster_ids // 128], axis=1).astype(
        jnp.float32
    )


def kernel_block(row_pts, row_nrm, col_pts, col_nrm):
    separation = row_pts[:, :, :, None] - col_pts[:, :, None, :]
    distance = jnp.sqrt(jnp.sum(separation * separation, axis=1))
    inverse = 1.0 / distance
    along_row = jnp.sum(separation * row_nrm[:, :, :, None], axis=1)
    along_col = jnp.sum(separation * col_nrm[:, :, None, :], axis=1)
    normal_dot = jnp.sum(row_nrm[:, :, :, None] * col_nrm[:, :, None, :], axis=1)
    green_value = inverse / (4.0 * math.pi)
    cosine = jnp.cos(wave_number * distance)
    sine_part = jnp.sin(wave_number * distance)
    slope_real = green_value * (-cosine * inverse - wave_number * sine_part)
    slope_imag = green_value * (-sine_part * inverse + wave_number * cosine)
    double_real = -along_col * inverse * slope_real
    double_imag = -along_col * inverse * slope_imag
    curve_real = 3.0 * inverse * inverse - wave_number * wave_number
    curve_imag = -3.0 * wave_number * inverse
    second_real = green_value * (cosine * curve_real - sine_part * curve_imag)
    second_imag = green_value * (sine_part * curve_real + cosine * curve_imag)
    tangle = along_row * along_col * inverse * inverse
    hyper_real = -(tangle * second_real + normal_dot * inverse * slope_real)
    hyper_imag = -(tangle * second_imag + normal_dot * inverse * slope_imag)
    return (double_real - hyper_imag / wave_number, double_imag + hyper_real / wave_number)


def sketch_pair(kern_real, kern_imag, right_block, left_block):
    halves = right_block.shape[1] // 2
    real_right = jnp.einsum("bak,bik->bai", right_block, kern_real, precision=precise)
    imag_right = jnp.einsum("bak,bik->bai", right_block, kern_imag, precision=precise)
    row_part = jnp.concatenate(
        [
            real_right[:, :halves] - imag_right[:, halves:],
            imag_right[:, :halves] + real_right[:, halves:],
        ],
        axis=1,
    )
    real_left = jnp.einsum("bai,bik->bak", left_block, kern_real, precision=precise)
    imag_left = jnp.einsum("bai,bik->bak", left_block, kern_imag, precision=precise)
    col_part = jnp.concatenate(
        [
            real_left[:, :halves] + imag_left[:, halves:],
            real_left[:, halves:] - imag_left[:, :halves],
        ],
        axis=1,
    )
    return (row_part, col_part)


def shards(
    point_offsets,
    panel_normals,
    right_sketch,
    left_sketch,
    pair_count,
    pair_rows,
    pair_offset,
    pair_cols,
):
    owners = lax.axis_size("clus")
    position = lax.axis_index("clus")
    cl_dev, width, panels = right_sketch.shape
    slots = pair_rows.shape[0]
    per_peer = max(2, 2 * slots // owners)
    slot_total = owners * per_peer
    local_ids = position * cl_dev + jnp.arange(cl_dev, dtype=jnp.int32)
    cluster_range = jnp.arange(cl_dev, dtype=jnp.int32)
    points = point_offsets + centers_of(local_ids)[:, :, None]
    live_count = pair_count[0]
    slot_index = jnp.arange(slots, dtype=jnp.int32)
    is_live = slot_index < live_count
    target = (position + 1 + pair_offset[:, 0]) % owners
    peer_hits = (target[:, None] == jnp.arange(owners, dtype=jnp.int32)[None, :]).astype(jnp.int32)
    peer_rank = jnp.sum(jnp.cumsum(peer_hits, axis=0) * peer_hits, axis=1) - 1
    send_pos = target * per_peer + peer_rank
    col_global = target * cl_dev + pair_cols
    zero_buffer = jnp.zeros((slot_total, width, panels), jnp.float32)
    zero_local = jnp.zeros((cl_dev, width, panels), jnp.float32)
    col_tags = (
        jnp.full((slot_total,), -1, jnp.int32).at[send_pos].set(jnp.where(is_live, pair_cols, -1))
    )
    incoming = lax.all_to_all(
        col_tags.reshape(owners, per_peer), "clus", split_axis=0, concat_axis=0, tiled=True
    ).reshape(slot_total)
    picked = jnp.maximum(incoming, 0)
    got_pts, got_nrm, got_right = (
        lax.all_to_all(
            point_offsets[picked].reshape(owners, per_peer, 3, panels),
            "clus",
            split_axis=0,
            concat_axis=0,
            tiled=True,
        ),
        lax.all_to_all(
            panel_normals[picked].reshape(owners, per_peer, 3, panels),
            "clus",
            split_axis=0,
            concat_axis=0,
            tiled=True,
        ),
        lax.all_to_all(
            right_sketch[picked].reshape(owners, per_peer, width, panels),
            "clus",
            split_axis=0,
            concat_axis=0,
            tiled=True,
        ),
    )
    got_pts = got_pts.reshape(slot_total, 3, panels)
    got_nrm = got_nrm.reshape(slot_total, 3, panels)
    got_right = got_right.reshape(slot_total, width, panels)

    def owner_step(block_turn, running):
        row_sum, outgoing = running
        block_index = block_turn * 8 + jnp.arange(8, dtype=jnp.int32)
        weight = (block_index < live_count).astype(jnp.float32)
        slot_at = lax.dynamic_slice_in_dim(send_pos, block_turn * 8, 8)
        row_local = lax.dynamic_slice_in_dim(pair_rows, block_turn * 8, 8)
        col_block = lax.dynamic_slice_in_dim(col_global, block_turn * 8, 8)
        col_pts = got_pts[slot_at] + centers_of(col_block)[:, :, None]
        kern_real, kern_imag = kernel_block(
            points[row_local], panel_normals[row_local], col_pts, got_nrm[slot_at]
        )
        row_part, col_part = sketch_pair(
            kern_real, kern_imag, got_right[slot_at], left_sketch[row_local]
        )
        select = (row_local[:, None] == cluster_range[None, :]).astype(jnp.float32) * weight[
            :, None
        ]
        row_sum = row_sum + jnp.einsum("bl,bak->lak", select, row_part, precision=precise)
        outgoing = outgoing.at[slot_at].add(col_part * weight[:, None, None])
        return (row_sum, outgoing)

    turn_count = (live_count + 7) // 8
    row_sum, outgoing = lax.fori_loop(0, turn_count, owner_step, (zero_local, zero_buffer))
    returned = lax.all_to_all(
        outgoing.reshape(owners, per_peer, width, panels),
        "clus",
        split_axis=0,
        concat_axis=0,
        tiled=True,
    ).reshape(slot_total, width, panels)
    select = (incoming[:, None] == cluster_range[None, :]).astype(jnp.float32)
    col_sum = jnp.einsum("sl,sak->lak", select, returned, precision=precise)
    return (row_sum, col_sum)


def solution(mesh):
    return jax.shard_map(
        shards,
        mesh=mesh,
        in_specs=(
            P(("groups", "clus"), None, None),
            P(("groups", "clus"), None, None),
            P(("groups", "clus"), None, None),
            P(("groups", "clus"), None, None),
            P(("groups", "clus")),
            P(("groups", "clus")),
            P(("groups", "clus"), None),
            P(("groups", "clus")),
        ),
        out_specs=(P(("groups", "clus"), None, None), P(("groups", "clus"), None, None)),
        check_vma=False,
    )
```

profile of v0, /device:TPU:15, one launch (start us, length us, event | category | flops | bytes accessed | tf_op | source)
XLA Modules:
  0.0 787.6 jit_solution(831881353410425316)
XLA Ops:
  4.9 10.2 %all_to_all.29 = s32[16,1,16]{2,1,0:T(1,128)S(1)} all-to-all(s32[16,1,16]{2,1,0:T(1,128)S(1)} %all_to_all.18), channel_id=1, replica_groups=mesh['groups'=2,'clus'=16] {'clus'}, dimensions={0} | all-to-all | bytes 2048 | tf_op jit(solution)/shard_map/all_to_all | solution.py:97
  19.1 6.1 all-to-all-start.3
  27.1 8.8 %all-to-all-done.3 = f32[16,16,3,128]{3,1,2,0:T(8,128)S(1)} async-done(((f32[16,16,3,128]{3,1,2,0:T(8,128)}), f32[16,16,3,128]{3,1,2,0:T(8,128)S(1)}, u32[]{:S(2)}, u32[]{:S(2)}) %all-to-all-start.3) | async-done | bytes 393248 | tf_op jit(solution)/shard_map/all_to_all | solution.py:109
  35.9 4.9 all-to-all-start.2
  40.9 4.3 gather_fusion.6
  45.2 6.4 all-to-all-done.2
  51.7 6.2 all-to-all-start.1
  60.6 179.6 %all-to-all-done.1 = f32[16,16,64,128]{3,2,1,0:T(8,128)} async-done(((f32[16,16,64,128]{3,2,1,0:T(8,128)}), f32[16,16,64,128]{3,2,1,0:T(8,128)}, u32[]{:S(2)}, u32[]{:S(2)}) %all-to-all-start.1) | async-done | bytes 8388640 | tf_op jit(solution)/shard_map/all_to_all | solution.py:116
  240.3 4.3 broadcast_in_dim.21
  244.5 334.5 %while.16 = (s32[]{:T(128)}, f32[16,64,128]{2,0,1:T(8,128)S(1)}, f32[256,64,128]{2,1,0:T(8,128)}, s32[]{:T(128)}, s32[128]{0:T(128)S(1)}, /*index=5*/s32[]{:T(12...) while((s32[]{:T(128)}, f32[16,64,128]{2,0,1:T(8,128)S(1)}, ...), condition=%wide.region_9.10_spmd.clone, body=%wide.region_3.9_spmd.clone.sunk | while | flops 424679168 | bytes 15386087 | solution.py:150
  250.7 3.9 gather_fusion
  255.8 2.8 multiply_add_fusion.2
  271.6 3.9 gather_fusion
  276.7 2.8 multiply_add_fusion.2
  292.5 3.9 gather_fusion
  297.6 2.8 multiply_add_fusion.2
  313.4 3.9 gather_fusion
  318.5 2.8 multiply_add_fusion.2
  334.3 3.9 gather_fusion
  339.5 2.8 multiply_add_fusion.2
  355.2 3.9 gather_fusion
  360.4 2.8 multiply_add_fusion.2
  376.2 3.9 gather_fusion
  381.3 2.8 multiply_add_fusion.2
  397.1 3.9 gather_fusion
  402.2 2.8 multiply_add_fusion.2
  409.6 2.3 scatter_fusion
  418.0 3.9 gather_fusion
  423.1 2.8 multiply_add_fusion.2
  438.9 3.9 gather_fusion
  444.0 2.8 multiply_add_fusion.2
  459.8 3.9 gather_fusion
  464.9 2.8 multiply_add_fusion.2
  480.7 3.9 gather_fusion
  485.8 2.8 multiply_add_fusion.2
  501.6 3.9 gather_fusion
  506.7 2.8 multiply_add_fusion.2
  522.5 3.9 gather_fusion
  527.6 2.8 multiply_add_fusion.2
  543.4 3.9 gather_fusion
  548.6 2.8 multiply_add_fusion.2
  564.3 3.9 gather_fusion
  569.5 2.8 multiply_add_fusion.2
  579.1 13.1 %copy.64 = f32[16,16,64,128]{3,1,2,0:T(8,128)} copy(f32[16,16,64,128]{3,2,1,0:T(8,128)} %bitcast.66) | data formatting | bytes 16777216 | tf_op jit(solution)/shard_map/reshape | solution.py:152
  592.2 4.8 all-to-all-start.4
  598.0 181.3 %all-to-all-done.4 = f32[16,16,64,128]{3,1,2,0:T(8,128)} async-done(((f32[16,16,64,128]{3,1,2,0:T(8,128)}), f32[16,16,64,128]{3,1,2,0:T(8,128)}, u32[]{:S(2)}, u32[]{:S(2)}) %all-to-all-start.4) | async-done | bytes 8388640 | tf_op jit(solution)/shard_map/all_to_all | solution.py:151
  779.3 4.4 copy.65
  783.7 2.9 fusion.19
  (440 shorter events, 236.7 us)
Async XLA Ops:
  0.6 40.2 %copy-start = (f32[16,64,128]{2,1,0:T(8,128)S(1)}, f32[16,64,128]{2,1,0:T(8,128)}, u32[]{:S(2)}) copy-start(f32[16,64,128]{2,1,0:T(8,128)} %param.12) | copy-start | bytes 1572868
  0.6 24.5 %copy-start.2 = (f32[16,3,128]{2,0,1:T(8,128)S(1)}, f32[16,3,128]{2,0,1:T(8,128)}, u32[]{:S(2)}) copy-start(f32[16,3,128]{2,0,1:T(8,128)} %param.10) | copy-start | bytes 73732
  19.1 16.9 %all-to-all-start.3 = ((f32[16,16,3,128]{3,1,2,0:T(8,128)}), f32[16,16,3,128]{3,1,2,0:T(8,128)S(1)}, u32[]{:S(2)}, u32[]{:S(2)}) async-start(f32[16,16,3,128]{3,1,2,0:T(8,128)} %copy.59), calls=%async_computation.3 | async-start | bytes 786432 | tf_op jit(solution)/shard_map/all_to_all | solution.py:109
  35.9 15.7 %all-to-all-start.2 = ((f32[16,16,3,128]{3,1,2,0:T(8,128)}), f32[16,16,3,128]{3,1,2,0:T(8,128)S(1)}, u32[]{:S(2)}, u32[]{:S(2)}) async-start(f32[16,16,3,128]{3,1,2,0:T(8,128)} %copy.57), calls=%async_computation.2 | async-start | bytes 786432 | tf_op jit(solution)/shard_map/all_to_all | solution.py:102
  51.7 6.2 copy-start.1
  51.7 188.6 %all-to-all-start.1 = ((f32[16,16,64,128]{3,2,1,0:T(8,128)}), f32[16,16,64,128]{3,2,1,0:T(8,128)}, u32[]{:S(2)}, u32[]{:S(2)}) async-start(f32[16,16,64,128]{3,2,1,0:T(8,128)} %bitcast.67), calls=%async_computation.1 | async-start | bytes 16777216 | tf_op jit(solution)/shard_map/all_to_all | solution.py:116
  57.9 186.7 %copy-start.3 = (f32[16,64,128]{2,1,0:T(8,128)S(1)}, f32[16,64,128]{2,1,0:T(8,128)}, u32[]{:S(2)}) copy-start(f32[16,64,128]{2,1,0:T(8,128)} %param.13) | copy-start | bytes 1572868
  57.9 186.7 %copy-start.4 = (s32[128]{0:T(128)S(1)}, s32[128]{0:T(128)}, u32[]{:S(2)}) copy-start(s32[128]{0:T(128)} %param.15) | copy-start | bytes 1540
  592.2 187.1 %all-to-all-start.4 = ((f32[16,16,64,128]{3,1,2,0:T(8,128)}), f32[16,16,64,128]{3,1,2,0:T(8,128)}, u32[]{:S(2)}, u32[]{:S(2)}) async-start(f32[16,16,64,128]{3,1,2,0:T(8,128)} %copy.64), calls=%async_computation.4 | async-start | bytes 16777216 | tf_op jit(solution)/shard_map/all_to_all | solution.py:151
where the time goes:
time: 793 us; the launch traced here: 788 us
  waiting for transfers between devices  376 us (47%)
  local copies, waits for them, and re-layouts  170 us (21%)
  other arithmetic  134 us (17%)
  matrix products  71.9 us (9%)
  starting transfers between devices  22 us (3%)
  blocking collectives  10.2 us (1%)
    all_to_all x1, waiting for transfers between devices, shards(): lax.all_to_all(outgoing.reshape(owners, per_peer, width, panels), 'clus',...  181 us
    all_to_all x1, waiting for transfers between devices, shards(): lax.all_to_all(right_sketch[picked].reshape(owners, per_peer, width, pane...  180 us
    gather x16, local copies, waits for them, and re-layouts, owner_step(): got_right[slot_at]  63.1 us
    add x16, other arithmetic, kernel_block(): double_imag + hyper_real / wave_number  44.6 us
    scatter-add x16, other arithmetic, owner_step(): outgoing = outgoing.at[slot_at].add(col_part * weight[:, None, None])  36 us
    gather x16, local copies, waits for them, and re-layouts, owner_step(): panel_normals[row_local]  21.3 us
    gather x16, local copies, waits for them, and re-layouts, owner_step(): points[row_local]  21.3 us
    reduce_sum x16, other arithmetic, kernel_block(): along_row = jnp.sum(separation * row_nrm[:, :, :, None], axis=1)  18.7 us
  transfers between devices with their start and end apart: 4, of which 4 were waited for; matrix products, arithmetic and copies ran while one was open for 1% of the time, Pallas kernels for 0%

commit v1 on v0

--- a/solution.py
+++ b/solution.py
@@ -2,7 +2,10 @@
 
 import jax
 import jax.numpy as jnp
+import numpy as np
 from jax import lax
+from jax.experimental import pallas as pl
+from jax.experimental.pallas import tpu as pltpu
 from jax.sharding import PartitionSpec as P
 
 wave_number = 8.0
@@ -62,7 +65,7 @@
     return (row_part, col_part)
 
 
-def shards(
+def exchange_shards(
     point_offsets,
     panel_normals,
     right_sketch,
@@ -160,6 +163,283 @@
     return (row_sum, col_sum)
 
 
+geometry_rows = 8
+unroll = 2
+vmem_budget = 40 * 2**20
+kernel_scale = wave_number * wave_number / (12.0 * math.pi)
+
+
+def phase_coefficients():
+    def fit(function, degree):
+        series = np.polynomial.chebyshev.Chebyshev.interpolate(function, degree, domain=[0.0, 0.25])
+        return [float(c) for c in series.convert(kind=np.polynomial.Polynomial).coef]
+
+    def sine_ratio(z):
+        return math.sqrt(2.0) * math.pi * np.sinc(np.sqrt(z))
+
+    def cosine(z):
+        return math.sqrt(2.0) * np.cos(math.pi * np.sqrt(z))
+
+    return fit(sine_ratio, 3), fit(cosine, 4)
+
+
+sine_terms, cosine_terms = phase_coefficients()
+
+
+def horner(terms, z):
+    value = terms[-1] * z + terms[-2]
+    for term in terms[-3::-1]:
+        value = value * z + term
+    return value
+
+
+def high_low(x):
+    high = lax.reduce_precision(x, 8, 7)
+    return high, lax.reduce_precision(x - high, 8, 7)
+
+
+def row_features(offsets, normals):
+    cl_dev, _, panels = offsets.shape
+    x = wave_number * jnp.swapaxes(offsets, 1, 2)
+    n = jnp.swapaxes(normals, 1, 2)
+    zero3 = jnp.zeros_like(x)
+    zero1 = zero3[:, :, :1]
+    one1 = jnp.ones_like(zero1)
+
+    def form(columns, constant):
+        high, low = high_low(jnp.concatenate(columns, axis=2))
+        c_high, rest = high_low(constant)
+        c_low = lax.reduce_precision(constant - c_high - rest, 8, 7)
+        tail = jnp.concatenate([c_high, rest, c_low, zero3, zero1, zero1], axis=2)
+        return jnp.concatenate([high, high, high, low, low, tail], axis=2)
+
+    square = form([-2.0 * x, zero3, one1, zero1], jnp.sum(x * x, axis=2, keepdims=True))
+    along_col = form([zero3, x, zero1, -one1], zero1)
+    along_row = form([-n, zero3, zero1, zero1], jnp.sum(x * n, axis=2, keepdims=True))
+    normal_dot = form([zero3, n, zero1, zero1], zero1)
+    top = jnp.concatenate([square, along_col], axis=2)
+    bottom = jnp.concatenate([along_row, normal_dot], axis=2)
+    return jnp.concatenate([top, bottom], axis=1).astype(jnp.bfloat16)
+
+
+def left_operand(left):
+    halves = left.shape[1] // 2
+    real, imag = left[:, :halves], left[:, halves:]
+    stacked = jnp.concatenate(
+        [jnp.concatenate([real, imag], axis=2), jnp.concatenate([imag, -real], axis=2)], axis=1
+    )
+    high, low = high_low(stacked)
+    return jnp.concatenate([high, low], axis=1).astype(jnp.bfloat16)
+
+
+def split_two(x):
+    high = x.astype(jnp.bfloat16)
+    return high, (x - high.astype(jnp.float32)).astype(jnp.bfloat16)
+
+
+def pair_parts(features, left, column, width, shift):
+    panels = column.shape[1]
+    halves = width // 2
+    geometry = column[width:]
+    index = lax.broadcasted_iota(jnp.int32, geometry.shape, 0)
+    move = jnp.where(
+        index == 0, shift[0], jnp.where(index == 1, shift[1], jnp.where(index == 2, shift[2], 0.0))
+    )
+    base = jnp.where(index < 3, wave_number, 1.0) * (geometry + move)
+    y = [base[i : i + 1] for i in range(3)]
+    m = [base[i : i + 1] for i in range(3, 6)]
+    square = y[0] * y[0] + y[1] * y[1] + y[2] * y[2]
+    inner = y[0] * m[0] + y[1] * m[1] + y[2] * m[2]
+    full = jnp.where(index == 6, square, jnp.where(index == 7, inner, base))
+    high = full.astype(jnp.bfloat16).astype(jnp.float32)
+    rest = full - high
+    middle = rest.astype(jnp.bfloat16).astype(jnp.float32)
+    low = rest - middle
+    stack = jnp.concatenate([high, middle, low, high, middle, jnp.ones_like(high)], axis=0).astype(
+        jnp.bfloat16
+    )
+    empty = jnp.zeros_like(stack)
+    operand = jnp.concatenate(
+        [jnp.concatenate([stack, empty], axis=1), jnp.concatenate([empty, stack], axis=1)], axis=0
+    )
+    forms = jnp.dot(features, operand, preferred_element_type=jnp.float32)
+
+    pieces = []
+    chunk = 32
+    magic = 1.5 * 2.0**23
+    for start in range(0, panels, chunk):
+        r2 = forms[start : start + chunk, :panels]
+        along_col = forms[start : start + chunk, panels:]
+        along_row = forms[panels + start : panels + start + chunk, :panels]
+        normal_dot = forms[panels + start : panels + start + chunk, panels:]
+        inverse = lax.rsqrt(r2)
+        turns = (r2 * inverse) * (0.5 / math.pi)
+        turns = turns - ((turns + magic) - magic)
+        z = turns * turns
+        sine_half = turns * horner(sine_terms, z)
+        cosine_half = horner(cosine_terms, z)
+        weight = 3.0 * (inverse * inverse)
+        scaled = sine_half * weight
+        sine_w = scaled * cosine_half
+        cosine_w = weight - scaled * sine_half
+        both = along_col * along_row
+        inner_term = normal_dot - both * weight
+        real = inner_term + along_col * inverse
+        imag = inverse * (inner_term + both) - along_col
+        pieces.append(
+            split_two(cosine_w * real - sine_w * imag) + split_two(cosine_w * imag + sine_w * real)
+        )
+    real_high, real_low, imag_high, imag_low = [
+        jnp.concatenate([piece[q] for piece in pieces], axis=0) for q in range(4)
+    ]
+    left_rhs = jnp.concatenate(
+        [
+            jnp.concatenate([real_high, real_low], axis=1),
+            jnp.concatenate([imag_high, imag_low], axis=1),
+        ],
+        axis=0,
+    )
+    right_rhs = jnp.concatenate(
+        [
+            jnp.concatenate([real_high, imag_high], axis=1),
+            jnp.concatenate([real_low, imag_low], axis=1),
+        ],
+        axis=0,
+    )
+    w_high, w_low = split_two(column[:width])
+
+    def complex_rows(block):
+        real, imag = block[:halves], block[halves:]
+        return [jnp.concatenate([real, -imag], axis=1), jnp.concatenate([imag, real], axis=1)]
+
+    right = jnp.concatenate(complex_rows(w_high) + complex_rows(w_low), axis=0)
+    row_out = lax.dot_general(
+        right, right_rhs, (((1,), (1,)), ((), ())), preferred_element_type=jnp.float32
+    )
+    col_out = jnp.dot(left, left_rhs, preferred_element_type=jnp.float32)
+
+    def fold(out):
+        return (
+            out[:width, :panels]
+            + out[:width, panels:]
+            + (out[width:, :panels] + out[width:, panels:])
+        )
+
+    return fold(row_out), fold(col_out)
+
+
+def pair_kernel(
+    live_ref, row_ref, global_row_ref, col_ref, features_ref, left_ref, column_ref, row_out, col_out
+):
+    row_out[...] = jnp.zeros_like(row_out)
+    width = row_out.shape[1]
+
+    def clear(i, carry):
+        col_out[i] = jnp.zeros(col_out.shape[1:], jnp.float32)
+        return carry
+
+    lax.fori_loop(0, col_out.shape[0], clear, 0)
+    live = live_ref[0]
+
+    def center(c):
+        return (c & 15, (c >> 4) & 7, c >> 7)
+
+    def turn(step, carry):
+        done = []
+        for k in range(unroll):
+            slot = step * unroll + k
+            row = row_ref[slot]
+            col = col_ref[slot]
+            shift = [
+                (b - a).astype(jnp.float32)
+                for a, b in zip(center(global_row_ref[slot]), center(col))
+            ]
+            parts = pair_parts(features_ref[row], left_ref[row], column_ref[col], width, shift)
+            scale = jnp.where(slot < live, kernel_scale, 0.0)
+            done.append((row, col, parts[0] * scale, parts[1] * scale))
+        for row, col, row_part, col_part in done:
+            row_out[row] += row_part
+            col_out[col] += col_part
+        return carry
+
+    lax.fori_loop(0, (live + unroll - 1) // unroll, turn, 0)
+
+
+def sketch_pairs(live, rows, global_rows, cols, features, left, columns, width):
+    cl_dev = features.shape[0]
+    clusters, _, panels = columns.shape
+    return pl.pallas_call(
+        pair_kernel,
+        grid_spec=pltpu.PrefetchScalarGridSpec(
+            num_scalar_prefetch=4,
+            in_specs=[pl.BlockSpec(memory_space=pltpu.VMEM)] * 3,
+            out_specs=[pl.BlockSpec(memory_space=pltpu.VMEM)] * 2,
+        ),
+        out_shape=(
+            jax.ShapeDtypeStruct((cl_dev, width, panels), jnp.float32),
+            jax.ShapeDtypeStruct((clusters, width, panels), jnp.float32),
+        ),
+        compiler_params=pltpu.CompilerParams(vmem_limit_bytes=vmem_budget),
+        name="pair_sketches",
+    )(live, rows, global_rows, cols, features, left, columns)
+
+
+def gather_shards(
+    point_offsets,
+    panel_normals,
+    right_sketch,
+    left_sketch,
+    pair_count,
+    pair_rows,
+    pair_offset,
+    pair_cols,
+):
+    owners = lax.axis_size("clus")
+    position = lax.axis_index("clus")
+    cl_dev, width, panels = right_sketch.shape
+    spare = jnp.zeros((cl_dev, geometry_rows - 6, panels), jnp.float32)
+    packed = jnp.concatenate([right_sketch, point_offsets, panel_normals, spare], axis=1)
+    columns = lax.all_gather(packed, "clus", axis=0, tiled=True)
+    target = (position + 1 + pair_offset[:, 0]) % owners
+    row_sum, outgoing = sketch_pairs(
+        pair_count,
+        pair_rows,
+        position * cl_dev + pair_rows,
+        target * cl_dev + pair_cols,
+        row_features(point_offsets, panel_normals),
+        left_operand(left_sketch),
+        columns,
+        width,
+    )
+    col_sum = lax.psum_scatter(outgoing, "clus", scatter_dimension=0, tiled=True)
+    return (row_sum, col_sum)
+
+
+def shards(
+    point_offsets,
+    panel_normals,
+    right_sketch,
+    left_sketch,
+    pair_count,
+    pair_rows,
+    pair_offset,
+    pair_cols,
+):
+    cl_dev, width, panels = right_sketch.shape
+    held = lax.axis_size("clus") * cl_dev * (2 * width + geometry_rows) * panels * 4
+    plan = gather_shards if held + 2**23 <= vmem_budget else exchange_shards
+    return plan(
+        point_offsets,
+        panel_normals,
+        right_sketch,
+        left_sketch,
+        pair_count,
+        pair_rows,
+        pair_offset,
+        pair_cols,
+    )
+
+
 def solution(mesh):
     return jax.shard_map(
         shards,

time: 793 us -> 264 us (0.33)
  the two profiles are of different devices: /device:TPU:15 before, /device:TPU:0 now
where the time goes in v1:
time: 264 us; the launch traced here: 263 us
  waiting for transfers between devices  141 us (53%)
  Pallas kernels  55.2 us (21%)
  local copies, waits for them, and re-layouts  36.3 us (14%)
  other arithmetic  15.8 us (6%)
  between operations  14.9 us (6%)
    reduce_scatter x1, waiting for transfers between devices, gather_shards(): lax.psum_scatter(outgoing, 'clus', scatter_dimension=0, tiled=True)  103 us
    pallas_call x1, Pallas kernels, sketch_pairs(): pl.pallas_call(pair_kernel, grid_spec=pltpu.PrefetchScalarGridSpec(num_sc...  55.2 us
    all_gather x1, waiting for transfers between devices, gather_shards(): columns = lax.all_gather(packed, 'clus', axis=0, tiled=True)  38.1 us
    another operation x5, other arithmetic  10.6 us
    concatenate x1, local copies, waits for them, and re-layouts, row_features(): top = jnp.concatenate([square, along_col], axis=2)  10.4 us
    concatenate x1, local copies, waits for them, and re-layouts, row_features(): bottom = jnp.concatenate([along_row, normal_dot], axis=2)  9.53 us
    unnamed x29, local copies, waits for them, and re-layouts  6.29 us
  transfers between devices with their start and end apart: 2, of which 2 were waited for; matrix products, arithmetic and copies ran while one was open for 17% of the time, Pallas kernels for 0%

profile of v1, /device:TPU:0, one launch (start us, length us, event | category | flops | bytes accessed | tf_op | source)
XLA Modules:
  0.0 263.4 jit_solution(15209145834646517158)
XLA Ops:
  7.2 0.0 all-gather.2.cloned.1.call-start
  7.2 0.8 copy.86
  8.0 0.8 copy.87
  8.8 0.1 pad.3.clone
  8.8 2.0 maximum_maximum_fusion.1
  10.8 0.0 all-gather.2.cloned.1.call-update
  10.8 0.0 reduce-scatter.2.cloned.1.call-start
  10.9 1.1 copy.82
  12.0 0.1 pad.17.clone
  12.1 0.4 copy.78
  12.4 1.5 multiply_reduce_fusion.1
  14.0 1.3 copy.84
  15.3 1.4 copy.83
  16.7 1.1 copy.85
  17.8 1.3 copy.80
  19.1 1.4 copy.79
  20.5 1.1 copy.81
  21.5 1.4 copy.77
  22.9 0.1 pad.21.clone
  23.0 0.1 pad.24.clone
  23.7 0.1 broadcast_in_dim.13
  23.8 0.0 copy-start.2
  23.9 3.5 %fusion.11 = (bf16[16,128,8]{2,1,0:T(8,128)(2,1)}, bf16[16,128,8]{2,1,0:T(8,128)(2,1)S(1)}, bf16[16,128,8]{2,1,0:T(8,128)(2,1)}, bf16[16,128,8]{2,1,0:T(8,128)(2,1)}) fusion(f32[16,128,3]{2,1,0:T(8,128)S(1)} %bitcast.20, f32[16,128,3]{2,1,0:T(8,128)S(1)} %broadcast_in_dim.13, f32[8]{0:T(128)S(1)} %pad.17.clone, f32[16,128,3]{2,1,0:T(8,128)} %get-tuple-element.24), kind=kLoop, calls=%fused_computation.29 | loop fusion | flops 229376 | bytes 204832 | tf_op jit(solution)/shard_map/convert.17
  27.4 1.3 fusion.9
  28.7 0.1 broadcast.59
  28.8 0.1 broadcast_in_dim.15
  28.9 0.1 slice.12
  29.0 9.5 %concatenate.45 = bf16[16,128,96]{2,1,0:T(8,128)(2,1)} concatenate(bf16[16,128,8]{2,1,0:T(8,128)(2,1)} %get-tuple-element.22, bf16[16,128,8]{2,1,0:T(8,128)(2,1)} %get-tuple-element.22, bf16[16,128,8]{2,1,0:T(8,128)(2,1)} %get-tuple-element.22, bf16[16,128,8]{2,1,0:T(8,128)(2,1)} %get-tuple-element.23, bf16[16,128,8]{2,1,0:T(8,128)(2,1)} %get-tuple-element.23, ...), dimensions={2} | concatenate | bytes 786432 | tf_op jit(solution)/shard_map/concatenate | solution.py:221
  38.5 0.1 slice.11
  38.6 4.3 %fusion.5 = (bf16[16,128,8]{2,1,0:T(8,128)(2,1)}, bf16[16,128,8]{2,1,0:T(8,128)(2,1)S(1)}, bf16[16,128,8]{2,1,0:T(8,128)(2,1)}, bf16[16,128,8]{2,1,0:T(8,128)(2,1)}) fusion(f32[16,128,1]{2,1,0:T(8,128)S(1)} %slice.11, f32[16,128,3]{2,1,0:T(8,128)S(1)} %bitcast.19, f32[16,128,3]{2,1,0:T(8,128)} %copy-done.2, f32[8]{0:T(128)S(1)} %pad.21.clone, ...), kind=kLoop, calls=%fused_computation.23 | loop fusion | flops 262144 | bytes 213056 | tf_op jit(solution)/shard_map/convert.37
  43.0 0.0 copy-start.4
  43.0 1.3 fusion.3
  44.3 10.4 %concatenate.42 = bf16[16,128,96]{2,1,0:T(8,128)(2,1)} concatenate(bf16[16,128,8]{2,1,0:T(8,128)(2,1)S(1)} %copy-done.3, bf16[16,128,8]{2,1,0:T(8,128)(2,1)S(1)} %copy-done.3, bf16[16,128,8]{2,1,0:T(8,128)(2,1)S(1)} %copy-done.3, bf16[16,128,8]{2,1,0:T(8,128)(2,1)} %get-tuple-element.17, bf16[16,128,8]{2,1,0:T(8,128)(2,1)} %get-tuple-element.17, bf16[16,128,1]{2,1,0:T(8,128)(2,1)} %copy.81, ...), dimensions={2} | concatenate | bytes 786432 | tf_op jit(solution)/shard_map/concatenate | solution.py:220
  54.7 1.6 pad_maximum_fusion.4.features_ref
  56.2 0.1 fusion.25
  56.3 0.0 copy-start.1
  56.4 0.0 copy-start.11
  56.4 0.0 copy-start.12
  56.4 0.2 reduce-precision_convert_fusion
  56.6 0.1 pad_maximum_fusion.5.left_ref
  56.7 0.3 copy-done.1
  57.0 0.0 copy-done.11
  57.0 0.0 copy-done.12
  57.1 38.1 %all-gather.2.cloned.1.call-done.column_ref = f32[256,72,128]{2,1,0:T(8,128)} async-done(((f32[16,72,128]{2,1,0:T(8,128)}), f32[256,72,128]{2,1,0:T(8,128)}) %all-gather.2.cloned.1.call-update) | async-done | bytes 9437200 | tf_op jit(solution)/shard_map/all_gather | solution.py:402
  95.1 55.2 %pair_sketches.1 = (f32[16,64,128]{2,1,0:T(8,128)}, f32[256,64,128]{2,1,0:T(8,128)S(1)}) custom-call(s32[1]{0:T(128)S(6)} %copy.88.live_ref, s32[128]{0:T(128)S(1)} %copy-done.1, s32[128]{0:T(128)S(1)} %get-tuple-element.39.global_row_ref, s32[128]{0:T(128)S(1)} %get-tuple-element.38.col_ref, bf16[16,256,96]{2,1,0:T(8,128)(2,1)S(1)} %pad_maximum_fusion.4.features_ref, ...), custom_call_target="tpu_custom_call" | custom-call | tf_op jit(solution)/shard_map/pair_sketches/pallas_call | solution.py:371
  150.3 3.2 %copy-done = f32[256,64,128]{2,1,0:T(8,128)} copy-done((f32[256,64,128]{2,1,0:T(8,128)}, f32[256,64,128]{2,1,0:T(8,128)S(1)}, u32[]{:S(2)}) %copy-start) | copy-done | bytes 8388632
  153.6 0.0 reduce-scatter.2.cloned.1.call-update
  153.6 102.9 %reduce-scatter.2.cloned.1.call-done = f32[16,64,128]{2,1,0:T(8,128)} async-done(((f32[256,64,128]{2,1,0:T(8,128)}), f32[16,64,128]{2,1,0:T(8,128)}) %reduce-scatter.2.cloned.1.call-update) | async-done | bytes 524304 | tf_op jit(solution)/shard_map/reduce_scatter | solution.py:414
  (21 shorter events, 0.1 us)
Async XLA Ops:
  7.2 4.9 %copy-start.10 = (f32[16,3,128]{2,0,1:T(8,128)S(1)}, f32[16,3,128]{2,0,1:T(8,128)}, u32[]{:S(2)}) copy-start(f32[16,3,128]{2,0,1:T(8,128)} %param.8) | copy-start | bytes 73732
  7.2 88.0 %all-gather.2.cloned.1.call-start = ((), (), s32[]{:S(2)}) async-start(), calls=%async_computation.1 | async-start | bytes 10027008 | tf_op jit(solution)/shard_map/all_gather | solution.py:402
  10.8 245.7 %reduce-scatter.2.cloned.1.call-start = ((), (), s32[]{:S(2)}) async-start(), calls=%async_computation.2 | async-start | bytes 8912896 | tf_op jit(solution)/shard_map/reduce_scatter | solution.py:414
  23.8 3.5 %copy-start.2 = (f32[16,128,3]{2,1,0:T(8,128)}, f32[16,128,3]{2,1,0:T(8,128)S(1)}, u32[]{:S(2)}) copy-start(f32[16,128,3]{2,1,0:T(8,128)S(1)} %broadcast_in_dim.13) | copy-start | bytes 73732
  23.8 3.5 %copy-start.7 = (f32[16,128,1]{2,1,0:T(8,128)S(1)}, f32[16,128,1]{2,1,0:T(8,128)}, u32[]{:S(2)}) copy-start(f32[16,128,1]{2,1,0:T(8,128)} %copy.84) | copy-start | bytes 24580
  23.9 3.5 %copy-start.8 = (f32[16,128,1]{2,1,0:T(8,128)S(1)}, f32[16,128,1]{2,1,0:T(8,128)}, u32[]{:S(2)}) copy-start(f32[16,128,1]{2,1,0:T(8,128)} %copy.83) | copy-start | bytes 24580
  38.6 4.4 %copy-start.5 = (f32[16,128,1]{2,1,0:T(8,128)S(1)}, f32[16,128,1]{2,1,0:T(8,128)}, u32[]{:S(2)}) copy-start(f32[16,128,1]{2,1,0:T(8,128)} %copy.80) | copy-start | bytes 24580
  38.6 4.3 %copy-start.6 = (f32[16,128,1]{2,1,0:T(8,128)S(1)}, f32[16,128,1]{2,1,0:T(8,128)}, u32[]{:S(2)}) copy-start(f32[16,128,1]{2,1,0:T(8,128)} %copy.79) | copy-start | bytes 24580
  43.0 1.3 copy-start.3
  43.0 1.3 copy-start.4
  54.7 1.6 copy-start.9
  56.3 0.7 copy-start.1
  56.4 0.7 copy-start.11
  56.4 0.7 copy-start.12
  150.3 3.2 %copy-start = (f32[256,64,128]{2,1,0:T(8,128)}, f32[256,64,128]{2,1,0:T(8,128)S(1)}, u32[]{:S(2)}) copy-start(f32[256,64,128]{2,1,0:T(8,128)S(1)} %get-tuple-element.5) | copy-start | bytes 25165828
Sparse Core Ops, SparseCore 0:
  10.9 84.1 all-gather.1
  153.7 102.7 reduce-scatter.1

commit v2 on v1

--- a/solution.py
+++ b/solution.py
@@ -1,3 +1,4 @@
+import functools
 import math
 
 import jax
@@ -193,48 +194,60 @@
     return value
 
 
-def high_low(x):
-    high = lax.reduce_precision(x, 8, 7)
-    return high, lax.reduce_precision(x - high, 8, 7)
-
-
-def row_features(offsets, normals):
-    cl_dev, _, panels = offsets.shape
-    x = wave_number * jnp.swapaxes(offsets, 1, 2)
-    n = jnp.swapaxes(normals, 1, 2)
-    zero3 = jnp.zeros_like(x)
-    zero1 = zero3[:, :, :1]
-    one1 = jnp.ones_like(zero1)
-
-    def form(columns, constant):
-        high, low = high_low(jnp.concatenate(columns, axis=2))
-        c_high, rest = high_low(constant)
-        c_low = lax.reduce_precision(constant - c_high - rest, 8, 7)
-        tail = jnp.concatenate([c_high, rest, c_low, zero3, zero1, zero1], axis=2)
-        return jnp.concatenate([high, high, high, low, low, tail], axis=2)
-
-    square = form([-2.0 * x, zero3, one1, zero1], jnp.sum(x * x, axis=2, keepdims=True))
-    along_col = form([zero3, x, zero1, -one1], zero1)
-    along_row = form([-n, zero3, zero1, zero1], jnp.sum(x * n, axis=2, keepdims=True))
-    normal_dot = form([zero3, n, zero1, zero1], zero1)
-    top = jnp.concatenate([square, along_col], axis=2)
-    bottom = jnp.concatenate([along_row, normal_dot], axis=2)
-    return jnp.concatenate([top, bottom], axis=1).astype(jnp.bfloat16)
-
-
-def left_operand(left):
-    halves = left.shape[1] // 2
-    real, imag = left[:, :halves], left[:, halves:]
-    stacked = jnp.concatenate(
-        [jnp.concatenate([real, imag], axis=2), jnp.concatenate([imag, -real], axis=2)], axis=1
-    )
-    high, low = high_low(stacked)
-    return jnp.concatenate([high, low], axis=1).astype(jnp.bfloat16)
-
-
 def split_two(x):
     high = x.astype(jnp.bfloat16)
     return high, (x - high.astype(jnp.float32)).astype(jnp.bfloat16)
+
+
+def rounded(x):
+    return x.astype(jnp.bfloat16).astype(jnp.float32)
+
+
+def row_features(geometry):
+    index = lax.broadcasted_iota(jnp.int32, geometry.shape, 0)
+    x = [wave_number * geometry[i : i + 1] for i in range(3)]
+    n = [geometry[i : i + 1] for i in range(3, 6)]
+    zero = jnp.zeros_like(x[0])
+    one = zero + 1.0
+
+    def rows(parts):
+        block = jnp.zeros_like(geometry)
+        for i, part in parts.items():
+            block = jnp.where(index == i, part, block)
+        return block
+
+    def form(parts, constant):
+        block = rows(parts)
+        high = rounded(block)
+        low = block - high
+        c_high = rounded(constant)
+        c_middle = rounded(constant - c_high)
+        tail = rows({0: c_high, 1: c_middle, 2: constant - c_high - c_middle})
+        return jnp.concatenate([high, high, high, low, low, tail], axis=0)
+
+    square = form(
+        {0: -2.0 * x[0], 1: -2.0 * x[1], 2: -2.0 * x[2], 6: one},
+        x[0] * x[0] + x[1] * x[1] + x[2] * x[2],
+    )
+    along_col = form({3: x[0], 4: x[1], 5: x[2], 7: -one}, zero)
+    along_row = form({0: -n[0], 1: -n[1], 2: -n[2]}, x[0] * n[0] + x[1] * n[1] + x[2] * n[2])
+    normal_dot = form({3: n[0], 4: n[1], 5: n[2]}, zero)
+    empty = jnp.zeros((32, geometry.shape[1]), jnp.float32)
+    left = jnp.concatenate([square, along_col, empty], axis=0)
+    right = jnp.concatenate([along_row, normal_dot, empty], axis=0)
+    both = jnp.concatenate([left.T, right.T], axis=0)
+    return both[:, :96].astype(jnp.bfloat16)
+
+
+def left_operand(left):
+    halves = left.shape[0] // 2
+
+    def complex_rows(block):
+        real, imag = block[:halves], block[halves:]
+        return [jnp.concatenate([real, imag], axis=1), jnp.concatenate([imag, -real], axis=1)]
+
+    high, low = split_two(left)
+    return jnp.concatenate(complex_rows(high) + complex_rows(low), axis=0)
 
 
 def pair_parts(features, left, column, width, shift):
@@ -384,6 +397,299 @@
     )(live, rows, global_rows, cols, features, left, columns)
 
 
+def neighbours(line):
+    me = lax.axis_index("clus")
+    core, side, place = me % 2, me // 2 % 2, me // 4
+    return me, core, side, place
+
+
+def index_of(place, side, core):
+    return place * 4 + side * 2 + core
+
+
+def greet(line, place, side, core):
+    barrier = pltpu.get_barrier_semaphore()
+
+    def call(target):
+        pl.semaphore_signal(barrier, inc=1, device_id={"clus": target})
+
+    call(index_of(place, side, 1 - core))
+    call(index_of(place, 1 - side, core))
+
+    @pl.when(place > 0)
+    def _():
+        call(index_of(place - 1, side, core))
+
+    @pl.when(place < line - 1)
+    def _():
+        call(index_of(place + 1, side, core))
+
+    pl.semaphore_wait(barrier, 2 + jnp.minimum(place, 1) + jnp.minimum(line - 1 - place, 1))
+
+
+def gather_kernel(
+    line,
+    x_ref,
+    sketch_ref,
+    out_ref,
+    features_ref,
+    left_ref,
+    send_sem,
+    recv_sem,
+    local_sem,
+):
+    me, core, side, place = neighbours(line)
+    size = x_ref.shape[0]
+
+    def block(q):
+        return out_ref.at[pl.ds(pl.multiple_of(q * size, size), size)]
+
+    def copy(q, target, index):
+        return pltpu.make_async_remote_copy(
+            src_ref=block(q),
+            dst_ref=block(q),
+            send_sem=send_sem.at[index],
+            recv_sem=recv_sem.at[q],
+            device_id={"clus": target},
+        )
+
+    def arrived(q):
+        copy(q, index_of(place, side, 1 - core), 0).wait_recv()
+
+    mine = pltpu.make_async_copy(x_ref, block(me), local_sem)
+    mine.start()
+    greet(line, place, side, core)
+    mine.wait()
+
+    sends = []
+
+    def send(condition, q, target):
+        sends.append((condition, q, target))
+        index = len(sends) - 1
+
+        @pl.when(condition)
+        def _():
+            copy(q, target, index).start()
+
+    always = place >= 0
+    sibling = index_of(place, side, 1 - core)
+    across = index_of(place, 1 - side, core)
+    down = index_of(place - 1, side, core)
+    up = index_of(place + 1, side, core)
+
+    def pass_on(q, here, forward, target):
+        send(here & forward, q, target)
+        send(here, q, across)
+        send(here, q, sibling)
+
+    def relay(q, here):
+        @pl.when(here)
+        def _():
+            arrived(q)
+
+        send(here, q, sibling)
+
+    send(place < line - 1, me, up)
+    send(place > 0, me, down)
+    send(always, me, across)
+    send(always, me, sibling)
+    width = sketch_ref.shape[1]
+
+    def prepare(i, carry):
+        features_ref[i] = row_features(x_ref[i][width:])
+        left_ref[i] = left_operand(sketch_ref[i])
+        return carry
+
+    lax.fori_loop(0, size, prepare, 0)
+    for step in range(1, line + 1):
+        if step < line:
+            below, above = place >= step, place + step < line
+            for here, z, forward, target in (
+                (below, place - step, place < line - 1, up),
+                (above, place + step, place > 0, down),
+            ):
+                q = index_of(z, side, core)
+
+                @pl.when(here)
+                def _(q=q):
+                    arrived(q)
+
+                pass_on(q, here, forward, target)
+        if step == 1:
+            relay(across, always)
+        else:
+            relay(index_of(place - step + 1, 1 - side, core), place >= step - 1)
+            relay(index_of(place + step - 1, 1 - side, core), place + step - 1 < line)
+    for z in range(line):
+        for s in range(2):
+            arrived(index_of(z, s, 1 - core))
+    for index, (condition, q, target) in enumerate(sends):
+
+        @pl.when(condition)
+        def _(index=index, q=q, target=target):
+            copy(q, target, index).wait_send()
+
+
+def gather_clusters(packed, left_sketch, owners):
+    line = owners // 4
+    cl_dev, width, panels = left_sketch.shape
+    shape = (owners * packed.shape[0],) + packed.shape[1:]
+    most = 4 + 3 * 2 * (line - 1) + 1 + 2 * (line - 1)
+    return pl.pallas_call(
+        functools.partial(gather_kernel, line),
+        out_shape=(
+            jax.ShapeDtypeStruct(shape, packed.dtype),
+            jax.ShapeDtypeStruct((cl_dev, 2 * panels, 96), jnp.bfloat16),
+            jax.ShapeDtypeStruct((cl_dev, 2 * width, 2 * panels), jnp.bfloat16),
+        ),
+        in_specs=[pl.BlockSpec(memory_space=pltpu.VMEM)] * 2,
+        out_specs=[pl.BlockSpec(memory_space=pltpu.VMEM)] * 3,
+        scratch_shapes=[
+            pltpu.SemaphoreType.DMA((most,)),
+            pltpu.SemaphoreType.DMA((owners,)),
+            pltpu.SemaphoreType.DMA,
+        ],
+        compiler_params=pltpu.CompilerParams(
+            collective_id=0, has_side_effects=True, vmem_limit_bytes=vmem_budget
+        ),
+        name="gather_clusters",
+    )(packed, left_sketch)
+
+
+def scatter_kernel(
+    line, x_ref, out_ref, core_buf, side_buf, low_buf, high_buf, send_sem, core_sem, side_sem, low_sem, high_sem
+):
+    me, core, side, place = neighbours(line)
+    size = out_ref.shape[0]
+
+    def block(q):
+        return x_ref.at[pl.ds(pl.multiple_of(q * size, size), size)]
+
+    half = place // 2
+    order = [3 - 3 * half, 2 - half, 1 - place + 4 * half, place]
+
+    def to_sibling(z, s, index):
+        return pltpu.make_async_remote_copy(
+            src_ref=block(index_of(z, s, 1 - core)),
+            dst_ref=core_buf.at[z * 2 + s],
+            send_sem=send_sem.at[index],
+            recv_sem=core_sem.at[z * 2 + s],
+            device_id={"clus": index_of(place, side, 1 - core)},
+        )
+
+    def to_side(z, index):
+        return pltpu.make_async_remote_copy(
+            src_ref=core_buf.at[z * 2 + 1 - side],
+            dst_ref=side_buf.at[z],
+            send_sem=send_sem.at[index],
+            recv_sem=side_sem.at[z],
+            device_id={"clus": index_of(place, 1 - side, core)},
+        )
+
+    def along(z, index, buf, sem, target):
+        return pltpu.make_async_remote_copy(
+            src_ref=side_buf.at[z],
+            dst_ref=buf.at[z],
+            send_sem=send_sem.at[index],
+            recv_sem=sem.at[z],
+            device_id={"clus": index_of(target, side, core)},
+        )
+
+    def upward(z, index):
+        return along(z, index, low_buf, low_sem, place + 1)
+
+    def downward(z, index):
+        return along(z, index, high_buf, high_sem, place - 1)
+
+    greet(line, place, side, core)
+    for k, z in enumerate(order):
+        for j, s in enumerate((1 - side, side)):
+            to_sibling(z, s, 2 * k + j).start()
+    for k, z in enumerate(order):
+        s = 1 - side
+        to_sibling(z, s, 2 * k).wait_recv()
+        core_buf[z * 2 + s] = core_buf[z * 2 + s] + block(index_of(z, s, core))[...]
+        to_side(z, 8 + k).start()
+    for k, z in enumerate(order):
+        to_sibling(z, side, 2 * k + 1).wait_recv()
+        core_buf[z * 2 + side] = core_buf[z * 2 + side] + block(index_of(z, side, core))[...]
+    for k, z in enumerate(order):
+        to_side(z, 8 + k).wait_recv()
+        side_buf[z] = side_buf[z] + core_buf[z * 2 + side]
+        if k < line - 1:
+
+            @pl.when((z > place) & (place > 0))
+            def _(z=z):
+                upward(z, 0).wait_recv()
+                side_buf[z] = side_buf[z] + low_buf[z]
+
+            @pl.when((z < place) & (place < line - 1))
+            def _(z=z):
+                downward(z, 0).wait_recv()
+                side_buf[z] = side_buf[z] + high_buf[z]
+
+            @pl.when(z > place)
+            def _(z=z, k=k):
+                upward(z, 12 + k).start()
+
+            @pl.when(z < place)
+            def _(z=z, k=k):
+                downward(z, 12 + k).start()
+
+    out_ref[...] = side_buf[place]
+
+    @pl.when(place > 0)
+    def _():
+        upward(place, 0).wait_recv()
+        out_ref[...] = out_ref[...] + low_buf[place]
+
+    @pl.when(place < line - 1)
+    def _():
+        downward(place, 0).wait_recv()
+        out_ref[...] = out_ref[...] + high_buf[place]
+
+    for k, z in enumerate(order):
+        for j, s in enumerate((1 - side, side)):
+            to_sibling(z, s, 2 * k + j).wait_send()
+        to_side(z, 8 + k).wait_send()
+        if k < line - 1:
+
+            @pl.when(z > place)
+            def _(z=z, k=k):
+                upward(z, 12 + k).wait_send()
+
+            @pl.when(z < place)
+            def _(z=z, k=k):
+                downward(z, 12 + k).wait_send()
+
+
+def scatter_sums(outgoing, owners):
+    line = owners // 4
+    clusters, width, panels = outgoing.shape
+    block = (clusters // owners, width, panels)
+    return pl.pallas_call(
+        functools.partial(scatter_kernel, line),
+        out_shape=jax.ShapeDtypeStruct(block, outgoing.dtype),
+        in_specs=[pl.BlockSpec(memory_space=pltpu.VMEM)],
+        out_specs=pl.BlockSpec(memory_space=pltpu.VMEM),
+        scratch_shapes=[
+            pltpu.VMEM((2 * line,) + block, jnp.float32),
+            pltpu.VMEM((line,) + block, jnp.float32),
+            pltpu.VMEM((line,) + block, jnp.float32),
+            pltpu.VMEM((line,) + block, jnp.float32),
+            pltpu.SemaphoreType.DMA((4 * line,)),
+            pltpu.SemaphoreType.DMA((2 * line,)),
+            pltpu.SemaphoreType.DMA((line,)),
+            pltpu.SemaphoreType.DMA((line,)),
+            pltpu.SemaphoreType.DMA((line,)),
+        ],
+        compiler_params=pltpu.CompilerParams(
+            collective_id=1, has_side_effects=True, vmem_limit_bytes=vmem_budget
+        ),
+        name="scatter_sums",
+    )(outgoing)
+
+
 def gather_shards(
     point_offsets,
     panel_normals,
@@ -399,19 +705,19 @@
     cl_dev, width, panels = right_sketch.shape
     spare = jnp.zeros((cl_dev, geometry_rows - 6, panels), jnp.float32)
     packed = jnp.concatenate([right_sketch, point_offsets, panel_normals, spare], axis=1)
-    columns = lax.all_gather(packed, "clus", axis=0, tiled=True)
+    columns, features, left = gather_clusters(packed, left_sketch, owners)
     target = (position + 1 + pair_offset[:, 0]) % owners
     row_sum, outgoing = sketch_pairs(
         pair_count,
         pair_rows,
         position * cl_dev + pair_rows,
         target * cl_dev + pair_cols,
-        row_features(point_offsets, panel_normals),
-        left_operand(left_sketch),
+        features,
+        left,
         columns,
         width,
     )
-    col_sum = lax.psum_scatter(outgoing, "clus", scatter_dimension=0, tiled=True)
+    col_sum = scatter_sums(outgoing, owners)
     return (row_sum, col_sum)
 
 
@@ -427,7 +733,8 @@
 ):
     cl_dev, width, panels = right_sketch.shape
     held = lax.axis_size("clus") * cl_dev * (2 * width + geometry_rows) * panels * 4
-    plan = gather_shards if held + 2**23 <= vmem_budget else exchange_shards
+    fits = lax.axis_size("clus") == 16 and held + 2**23 <= vmem_budget
+    plan = gather_shards if fits else exchange_shards
     return plan(
         point_offsets,
         panel_normals,

time: 264 us -> 180 us (0.68)
  waiting for transfers between devices: 141 us -> 0 us
  Pallas kernels: 55.2 us -> 170 us
  local copies, waits for them, and re-layouts: 36.3 us -> 7.68 us
  other arithmetic: 15.8 us -> 1.86 us
  between operations: 14.9 us -> 1.33 us
    pallas_call x0 -> x2, Pallas kernels: none -> 137 us  [the longest x1 75.7 us: scatter_sums(): pl.pallas_call(functools.partial(scatter_kernel, line), out_shape=jax.Sha...]
    reduce_scatter x1 -> x0, waiting for transfers between devices: 103 us -> none  [gather_shards(): lax.psum_scatter(outgoing, 'clus', scatter_dimension=0, tiled=True)]
    all_gather x1 -> x0, waiting for transfers between devices: 38.1 us -> none  [gather_shards(): columns = lax.all_gather(packed, 'clus', axis=0, tiled=True)]
    pallas_call x1, Pallas kernels: 55.2 us -> 33.9 us  [sketch_pairs(): pl.pallas_call(pair_kernel, grid_spec=pltpu.PrefetchScalarGridSpec(num_sc...]
    concatenate x5 -> x0, local copies, waits for them, and re-layouts: 20.2 us -> none  [the longest x1 10.4 us: row_features(): top = jnp.concatenate([square, along_col], axis=2)]
    another operation x5 -> x0, other arithmetic: 10.6 us -> none
    reduce_sum x2 -> x0, local copies, waits for them, and re-layouts: 2.73 us -> none  [the longest x1 1.37 us: row_features(): jnp.sum(x * x, axis=2, keepdims=True)]
    reduce_precision x2 -> x0, local copies, waits for them, and re-layouts: 2.69 us -> none  [high_low(): high = lax.reduce_precision(x, 8, 7)]
  transfers between devices with their start and end apart: 2 -> 0, of which waited for: 2 -> 0; matrix products, arithmetic and copies ran while one was open for 17% -> 0% of each run, Pallas kernels for 0% -> 0%
where the time goes in v2:
time: 180 us; the launch traced here: 181 us
  Pallas kernels  170 us (94%)
  local copies, waits for them, and re-layouts  7.68 us (4%)
  other arithmetic  1.86 us (1%)
    pallas_call x1, Pallas kernels, scatter_sums(): pl.pallas_call(functools.partial(scatter_kernel, line), out_shape=jax.Sha...  75.7 us
    pallas_call x1, Pallas kernels, gather_clusters(): pl.pallas_call(functools.partial(gather_kernel, line), out_shape=(jax.Sha...  60.9 us
    pallas_call x1, Pallas kernels, sketch_pairs(): pl.pallas_call(pair_kernel, grid_spec=pltpu.PrefetchScalarGridSpec(num_sc...  33.9 us
    unnamed x9, local copies, waits for them, and re-layouts  7.6 us

profile of v2, /device:TPU:0, one launch (start us, length us, event | category | flops | bytes accessed | tf_op | source)
XLA Modules:
  0.0 181.3 jit_solution(5537193048879322709)
XLA Ops:
  1.3 0.7 fusion.1
  2.0 0.1 pad.3.clone
  2.1 0.8 copy.10
  2.8 0.8 copy.11
  3.6 1.2 maximum_maximum_fusion.x_ref
  4.7 0.0 copy-start.1
  4.7 1.0 copy-done.1
  5.8 60.9 %gather_clusters.1 = (f32[256,72,128]{2,1,0:T(8,128)S(1)}, bf16[16,256,96]{2,1,0:T(8,128)(2,1)S(1)}, bf16[16,128,256]{2,1,0:T(8,128)(2,1)S(1)}) custom-call(f32[16,72,128]{2,1,0:T(8,128)S(1)} %maximum_maximum_fusion.x_ref, f32[16,64,128]{2,1,0:T(8,128)S(1)} %copy-done.1), custom_call_target="tpu_custom_call" | custom-call | tf_op jit(solution)/shard_map/gather_clusters/pallas_call | solution.py:538
  66.6 0.0 copy-start
  66.7 3.6 %copy-done = f32[256,72,128]{2,1,0:T(8,128)} copy-done((f32[256,72,128]{2,1,0:T(8,128)}, f32[256,72,128]{2,1,0:T(8,128)S(1)}, u32[]{:S(2)}) %copy-start) | copy-done | bytes 9437208
  70.3 0.0 copy-start.2
  70.3 0.7 copy-done.2
  70.9 33.9 %pair_sketches.1 = (f32[16,64,128]{2,1,0:T(8,128)}, f32[256,64,128]{2,1,0:T(8,128)S(1)}) custom-call(s32[1]{0:T(128)S(6)} %copy.13.live_ref, s32[128]{0:T(128)S(1)} %copy-done.2, s32[128]{0:T(128)S(1)} %get-tuple-element.13.global_row_ref, s32[128]{0:T(128)S(1)} %get-tuple-element.12.col_ref, bf16[16,256,96]{2,1,0:T(8,128)(2,1)S(1)} %get-tuple-element.7.features_ref, ...), custom_call_target="tpu_custom_call" | custom-call | tf_op jit(solution)/shard_map/pair_sketches/pallas_call | solution.py:384
  104.8 75.7 %scatter_sums.1 = f32[16,64,128]{2,1,0:T(8,128)S(1)} custom-call(f32[256,64,128]{2,1,0:T(8,128)S(1)} %get-tuple-element.11.x_ref), custom_call_target="tpu_custom_call" | custom-call | tf_op jit(solution)/shard_map/scatter_sums/pallas_call | solution.py:670
  180.5 0.8 copy.14
  (1 shorter events, 0.0 us)
Async XLA Ops:
  4.7 1.0 copy-start.1
  66.6 3.6 %copy-start = (f32[256,72,128]{2,1,0:T(8,128)}, f32[256,72,128]{2,1,0:T(8,128)S(1)}, u32[]{:S(2)}) copy-start(f32[256,72,128]{2,1,0:T(8,128)S(1)} %get-tuple-element.9.column_ref) | copy-start | bytes 28311556
  70.3 0.7 copy-start.2

commit v3 on v2

--- a/solution.py
+++ b/solution.py
@@ -165,7 +165,7 @@
 
 
 geometry_rows = 8
-unroll = 2
+unroll = 8
 vmem_budget = 40 * 2**20
 kernel_scale = wave_number * wave_number / (12.0 * math.pi)
 
@@ -299,26 +299,15 @@
         inner_term = normal_dot - both * weight
         real = inner_term + along_col * inverse
         imag = inverse * (inner_term + both) - along_col
-        pieces.append(
-            split_two(cosine_w * real - sine_w * imag) + split_two(cosine_w * imag + sine_w * real)
+        pieces.append((cosine_w * real - sine_w * imag, cosine_w * imag + sine_w * real))
+    real, imag = [jnp.concatenate([piece[q] for piece in pieces], axis=0) for q in range(2)]
+
+    def operand_of(real, imag):
+        return jnp.concatenate(
+            [jnp.concatenate(split_two(real), axis=1), jnp.concatenate(split_two(imag), axis=1)],
+            axis=0,
         )
-    real_high, real_low, imag_high, imag_low = [
-        jnp.concatenate([piece[q] for piece in pieces], axis=0) for q in range(4)
-    ]
-    left_rhs = jnp.concatenate(
-        [
-            jnp.concatenate([real_high, real_low], axis=1),
-            jnp.concatenate([imag_high, imag_low], axis=1),
-        ],
-        axis=0,
-    )
-    right_rhs = jnp.concatenate(
-        [
-            jnp.concatenate([real_high, imag_high], axis=1),
-            jnp.concatenate([real_low, imag_low], axis=1),
-        ],
-        axis=0,
-    )
+
     w_high, w_low = split_two(column[:width])
 
     def complex_rows(block):
@@ -326,10 +315,8 @@
         return [jnp.concatenate([real, -imag], axis=1), jnp.concatenate([imag, real], axis=1)]
 
     right = jnp.concatenate(complex_rows(w_high) + complex_rows(w_low), axis=0)
-    row_out = lax.dot_general(
-        right, right_rhs, (((1,), (1,)), ((), ())), preferred_element_type=jnp.float32
-    )
-    col_out = jnp.dot(left, left_rhs, preferred_element_type=jnp.float32)
+    row_out = jnp.dot(right, operand_of(real.T, imag.T), preferred_element_type=jnp.float32)
+    col_out = jnp.dot(left, operand_of(real, imag), preferred_element_type=jnp.float32)
 
     def fold(out):
         return (

time: 180 us -> 155 us (0.86); the launches traced: 181 us -> 153 us
  Pallas kernels: 170 us -> 143 us
    pallas_call x1, Pallas kernels: 75.7 us -> 60.4 us  [scatter_sums(): pl.pallas_call(functools.partial(scatter_kernel, line), out_shape=jax.Sha...]
    pallas_call x1, Pallas kernels: 33.9 us -> 21.2 us  [sketch_pairs(): pl.pallas_call(pair_kernel, grid_spec=pltpu.PrefetchScalarGridSpec(num_sc...]
where the time goes in v3:
time: 155 us; the launch traced here: 153 us
  Pallas kernels  143 us (92%)
  local copies, waits for them, and re-layouts  7.68 us (5%)
  other arithmetic  1.86 us (1%)
    pallas_call x1, Pallas kernels, gather_clusters(): pl.pallas_call(functools.partial(gather_kernel, line), out_shape=(jax.Sha...  60.9 us
    pallas_call x1, Pallas kernels, scatter_sums(): pl.pallas_call(functools.partial(scatter_kernel, line), out_shape=jax.Sha...  60.4 us
    pallas_call x1, Pallas kernels, sketch_pairs(): pl.pallas_call(pair_kernel, grid_spec=pltpu.PrefetchScalarGridSpec(num_sc...  21.2 us
    unnamed x9, local copies, waits for them, and re-layouts  7.6 us

profile of v3, /device:TPU:0, one launch (start us, length us, event | category | flops | bytes accessed | tf_op | source)
XLA Modules:
  0.0 153.4 jit_solution(1649615418107917244)
XLA Ops:
  1.3 0.7 fusion.1
  2.0 0.1 pad.3.clone
  2.1 0.8 copy.10
  2.8 0.8 copy.11
  3.6 1.2 maximum_maximum_fusion.x_ref
  4.7 0.0 copy-start.1
  4.7 1.0 copy-done.1
  5.8 60.9 %gather_clusters.1 = (f32[256,72,128]{2,1,0:T(8,128)S(1)}, bf16[16,256,96]{2,1,0:T(8,128)(2,1)S(1)}, bf16[16,128,256]{2,1,0:T(8,128)(2,1)S(1)}) custom-call(f32[16,72,128]{2,1,0:T(8,128)S(1)} %maximum_maximum_fusion.x_ref, f32[16,64,128]{2,1,0:T(8,128)S(1)} %copy-done.1), custom_call_target="tpu_custom_call" | custom-call | tf_op jit(solution)/shard_map/gather_clusters/pallas_call | solution.py:525
  66.6 0.0 copy-start
  66.7 3.6 %copy-done = f32[256,72,128]{2,1,0:T(8,128)} copy-done((f32[256,72,128]{2,1,0:T(8,128)}, f32[256,72,128]{2,1,0:T(8,128)S(1)}, u32[]{:S(2)}) %copy-start) | copy-done | bytes 9437208
  70.3 0.0 copy-start.2
  70.3 0.7 copy-done.2
  70.9 21.2 %pair_sketches.1 = (f32[16,64,128]{2,1,0:T(8,128)}, f32[256,64,128]{2,1,0:T(8,128)S(1)}) custom-call(s32[1]{0:T(128)S(6)} %copy.13.live_ref, s32[128]{0:T(128)S(1)} %copy-done.2, s32[128]{0:T(128)S(1)} %get-tuple-element.13.global_row_ref, s32[128]{0:T(128)S(1)} %get-tuple-element.12.col_ref, bf16[16,256,96]{2,1,0:T(8,128)(2,1)S(1)} %get-tuple-element.7.features_ref, ...), custom_call_target="tpu_custom_call" | custom-call | tf_op jit(solution)/shard_map/pair_sketches/pallas_call | solution.py:371
  92.2 60.4 %scatter_sums.1 = f32[16,64,128]{2,1,0:T(8,128)S(1)} custom-call(f32[256,64,128]{2,1,0:T(8,128)S(1)} %get-tuple-element.11.x_ref), custom_call_target="tpu_custom_call" | custom-call | tf_op jit(solution)/shard_map/scatter_sums/pallas_call | solution.py:657
  152.6 0.8 copy.14
  (1 shorter events, 0.0 us)
Async XLA Ops:
  4.7 1.0 copy-start.1
  66.6 3.6 %copy-start = (f32[256,72,128]{2,1,0:T(8,128)}, f32[256,72,128]{2,1,0:T(8,128)S(1)}, u32[]{:S(2)}) copy-start(f32[256,72,128]{2,1,0:T(8,128)S(1)} %get-tuple-element.9.column_ref) | copy-start | bytes 28311556
  70.3 0.7 copy-start.2

commit v4 on v3

--- a/solution.py
+++ b/solution.py
@@ -427,36 +427,36 @@
 ):
     me, core, side, place = neighbours(line)
     size = x_ref.shape[0]
-
-    def block(q):
-        return out_ref.at[pl.ds(pl.multiple_of(q * size, size), size)]
-
-    def copy(q, target, index):
+    part = size // 2
+
+    def block(q, half):
+        return out_ref.at[pl.ds(pl.multiple_of(q * size + half * part, part), part)]
+
+    def copy(q, half, target, index, own=False):
         return pltpu.make_async_remote_copy(
-            src_ref=block(q),
-            dst_ref=block(q),
+            src_ref=x_ref.at[pl.ds(half * part, part)] if own else block(q, half),
+            dst_ref=block(q, half),
             send_sem=send_sem.at[index],
-            recv_sem=recv_sem.at[q],
+            recv_sem=recv_sem.at[q * 2 + half],
             device_id={"clus": target},
         )
 
-    def arrived(q):
-        copy(q, index_of(place, side, 1 - core), 0).wait_recv()
-
-    mine = pltpu.make_async_copy(x_ref, block(me), local_sem)
+    def arrived(q, half):
+        copy(q, half, index_of(place, side, 1 - core), 0).wait_recv()
+
+    mine = pltpu.make_async_copy(x_ref, out_ref.at[pl.ds(pl.multiple_of(me * size, size), size)], local_sem)
     mine.start()
     greet(line, place, side, core)
-    mine.wait()
 
     sends = []
 
-    def send(condition, q, target):
-        sends.append((condition, q, target))
+    def send(condition, q, half, target, own=False):
+        sends.append((condition, q, half, target, own))
         index = len(sends) - 1
 
         @pl.when(condition)
         def _():
-            copy(q, target, index).start()
+            copy(q, half, target, index, own).start()
 
     always = place >= 0
     sibling = index_of(place, side, 1 - core)
@@ -464,22 +464,28 @@
     down = index_of(place - 1, side, core)
     up = index_of(place + 1, side, core)
 
-    def pass_on(q, here, forward, target):
-        send(here & forward, q, target)
-        send(here, q, across)
-        send(here, q, sibling)
-
-    def relay(q, here):
+    def pass_on(q, half, here, forward, target):
         @pl.when(here)
         def _():
-            arrived(q)
-
-        send(here, q, sibling)
-
-    send(place < line - 1, me, up)
-    send(place > 0, me, down)
-    send(always, me, across)
-    send(always, me, sibling)
+            arrived(q, half)
+
+        send(here & forward, q, half, target)
+        send(here, q, half, across)
+        send(here, q, half, sibling)
+
+    def relay(q, half, here):
+        @pl.when(here)
+        def _():
+            arrived(q, half)
+
+        send(here, q, half, sibling)
+
+    for half in range(2):
+        send(place < line - 1, me, half, up, True)
+        send(place > 0, me, half, down, True)
+        send(always, me, half, across, True)
+    for half in range(2):
+        send(always, me, half, sibling, True)
     width = sketch_ref.shape[1]
 
     def prepare(i, carry):
@@ -489,39 +495,37 @@
 
     lax.fori_loop(0, size, prepare, 0)
     for step in range(1, line + 1):
-        if step < line:
-            below, above = place >= step, place + step < line
-            for here, z, forward, target in (
-                (below, place - step, place < line - 1, up),
-                (above, place + step, place > 0, down),
-            ):
-                q = index_of(z, side, core)
-
-                @pl.when(here)
-                def _(q=q):
-                    arrived(q)
-
-                pass_on(q, here, forward, target)
-        if step == 1:
-            relay(across, always)
-        else:
-            relay(index_of(place - step + 1, 1 - side, core), place >= step - 1)
-            relay(index_of(place + step - 1, 1 - side, core), place + step - 1 < line)
+        for half in range(2):
+            if step < line:
+                pass_on(
+                    index_of(place - step, side, core), half, place >= step, place < line - 1, up
+                )
+                pass_on(
+                    index_of(place + step, side, core), half, place + step < line, place > 0, down
+                )
+            if step == 1:
+                relay(across, half, always)
+            else:
+                relay(index_of(place - step + 1, 1 - side, core), half, place >= step - 1)
+                relay(index_of(place + step - 1, 1 - side, core), half, place + step - 1 < line)
     for z in range(line):
         for s in range(2):
-            arrived(index_of(z, s, 1 - core))
-    for index, (condition, q, target) in enumerate(sends):
+            for half in range(2):
+                arrived(index_of(z, s, 1 - core), half)
+    for index, (condition, q, half, target, own) in enumerate(sends):
 
         @pl.when(condition)
-        def _(index=index, q=q, target=target):
-            copy(q, target, index).wait_send()
+        def _(index=index, q=q, half=half, target=target, own=own):
+            copy(q, half, target, index, own).wait_send()
+
+    mine.wait()
 
 
 def gather_clusters(packed, left_sketch, owners):
     line = owners // 4
     cl_dev, width, panels = left_sketch.shape
     shape = (owners * packed.shape[0],) + packed.shape[1:]
-    most = 4 + 3 * 2 * (line - 1) + 1 + 2 * (line - 1)
+    most = 2 * (4 + 3 * 2 * (line - 1) + 1 + 2 * (line - 1))
     return pl.pallas_call(
         functools.partial(gather_kernel, line),
         out_shape=(
@@ -530,10 +534,10 @@
             jax.ShapeDtypeStruct((cl_dev, 2 * width, 2 * panels), jnp.bfloat16),
         ),
         in_specs=[pl.BlockSpec(memory_space=pltpu.VMEM)] * 2,
-        out_specs=[pl.BlockSpec(memory_space=pltpu.VMEM)] * 3,
+        out_specs=[pl.BlockSpec(memory_space=pl.ANY)] + [pl.BlockSpec(memory_space=pltpu.VMEM)] * 2,
         scratch_shapes=[
             pltpu.SemaphoreType.DMA((most,)),
-            pltpu.SemaphoreType.DMA((owners,)),
+            pltpu.SemaphoreType.DMA((2 * owners,)),
             pltpu.SemaphoreType.DMA,
         ],
         compiler_params=pltpu.CompilerParams(
@@ -544,7 +548,20 @@
 
 
 def scatter_kernel(
-    line, x_ref, out_ref, core_buf, side_buf, low_buf, high_buf, send_sem, core_sem, side_sem, low_sem, high_sem
+    line,
+    x_ref,
+    out_ref,
+    own_buf,
+    core_buf,
+    side_buf,
+    low_buf,
+    high_buf,
+    send_sem,
+    own_sem,
+    core_sem,
+    side_sem,
+    low_sem,
+    high_sem,
 ):
     me, core, side, place = neighbours(line)
     size = out_ref.shape[0]
@@ -588,18 +605,28 @@
     def downward(z, index):
         return along(z, index, high_buf, high_sem, place - 1)
 
+    def fetch(z, s):
+        return pltpu.make_async_copy(
+            block(index_of(z, s, core)), own_buf.at[z * 2 + s], own_sem.at[z * 2 + s]
+        )
+
     greet(line, place, side, core)
     for k, z in enumerate(order):
-        for j, s in enumerate((1 - side, side)):
-            to_sibling(z, s, 2 * k + j).start()
+        to_sibling(z, 1 - side, 2 * k).start()
+        fetch(z, 1 - side).start()
+    for k, z in enumerate(order):
+        to_sibling(z, side, 2 * k + 1).start()
+        fetch(z, side).start()
     for k, z in enumerate(order):
         s = 1 - side
+        fetch(z, s).wait()
         to_sibling(z, s, 2 * k).wait_recv()
-        core_buf[z * 2 + s] = core_buf[z * 2 + s] + block(index_of(z, s, core))[...]
+        core_buf[z * 2 + s] = core_buf[z * 2 + s] + own_buf[z * 2 + s]
         to_side(z, 8 + k).start()
     for k, z in enumerate(order):
+        fetch(z, side).wait()
         to_sibling(z, side, 2 * k + 1).wait_recv()
-        core_buf[z * 2 + side] = core_buf[z * 2 + side] + block(index_of(z, side, core))[...]
+        core_buf[z * 2 + side] = core_buf[z * 2 + side] + own_buf[z * 2 + side]
     for k, z in enumerate(order):
         to_side(z, 8 + k).wait_recv()
         side_buf[z] = side_buf[z] + core_buf[z * 2 + side]
@@ -657,14 +684,16 @@
     return pl.pallas_call(
         functools.partial(scatter_kernel, line),
         out_shape=jax.ShapeDtypeStruct(block, outgoing.dtype),
-        in_specs=[pl.BlockSpec(memory_space=pltpu.VMEM)],
+        in_specs=[pl.BlockSpec(memory_space=pl.ANY)],
         out_specs=pl.BlockSpec(memory_space=pltpu.VMEM),
         scratch_shapes=[
+            pltpu.VMEM((2 * line,) + block, jnp.float32),
             pltpu.VMEM((2 * line,) + block, jnp.float32),
             pltpu.VMEM((line,) + block, jnp.float32),
             pltpu.VMEM((line,) + block, jnp.float32),
             pltpu.VMEM((line,) + block, jnp.float32),
             pltpu.SemaphoreType.DMA((4 * line,)),
+            pltpu.SemaphoreType.DMA((2 * line,)),
             pltpu.SemaphoreType.DMA((2 * line,)),
             pltpu.SemaphoreType.DMA((line,)),
             pltpu.SemaphoreType.DMA((line,)),

time: 155 us -> 155 us (level)
  the two profiles are of different devices: /device:TPU:0 before, /device:TPU:4 now
where the time goes in v4:
time: 155 us; the launch traced here: 154 us
  Pallas kernels  143 us (92%)
  local copies, waits for them, and re-layouts  7.68 us (5%)
  other arithmetic  1.86 us (1%)
    pallas_call x1, Pallas kernels, scatter_sums(): pl.pallas_call(functools.partial(scatter_kernel, line), out_shape=jax.Sha...  76.5 us
    pallas_call x1, Pallas kernels, gather_clusters(): pl.pallas_call(functools.partial(gather_kernel, line), out_shape=(jax.Sha...  55.2 us
    pallas_call x1, Pallas kernels, sketch_pairs(): pl.pallas_call(pair_kernel, grid_spec=pltpu.PrefetchScalarGridSpec(num_sc...  11 us
    unnamed x9, local copies, waits for them, and re-layouts  7.6 us

profile of v4, /device:TPU:4, one launch (start us, length us, event | category | flops | bytes accessed | tf_op | source)
XLA Modules:
  0.0 153.6 jit_solution(2586253995564925734)
XLA Ops:
  1.3 0.7 fusion.1
  2.0 0.1 pad.3.clone
  2.1 0.8 copy.10
  2.8 0.8 copy.11
  3.6 1.2 maximum_maximum_fusion.x_ref
  4.7 0.0 copy-start.1
  4.7 1.0 copy-done.1
  5.8 55.2 %gather_clusters.1 = (f32[256,72,128]{2,1,0:T(8,128)S(1)}, bf16[16,256,96]{2,1,0:T(8,128)(2,1)S(1)}, bf16[16,128,256]{2,1,0:T(8,128)(2,1)S(1)}) custom-call(f32[16,72,128]{2,1,0:T(8,128)S(1)} %maximum_maximum_fusion.x_ref, f32[16,64,128]{2,1,0:T(8,128)S(1)} %copy-done.1), custom_call_target="tpu_custom_call" | custom-call | tf_op jit(solution)/shard_map/gather_clusters/pallas_call | solution.py:529
  61.0 0.0 copy-start
  61.0 3.6 %copy-done = f32[256,72,128]{2,1,0:T(8,128)} copy-done((f32[256,72,128]{2,1,0:T(8,128)}, f32[256,72,128]{2,1,0:T(8,128)S(1)}, u32[]{:S(2)}) %copy-start) | copy-done | bytes 9437208
  64.6 0.0 copy-start.2
  64.6 0.7 copy-done.2
  65.3 11.0 %pair_sketches.1 = (f32[16,64,128]{2,1,0:T(8,128)}, f32[256,64,128]{2,1,0:T(8,128)S(1)}) custom-call(s32[1]{0:T(128)S(6)} %copy.13.live_ref, s32[128]{0:T(128)S(1)} %copy-done.2, s32[128]{0:T(128)S(1)} %get-tuple-element.13.global_row_ref, s32[128]{0:T(128)S(1)} %get-tuple-element.12.col_ref, bf16[16,256,96]{2,1,0:T(8,128)(2,1)S(1)} %get-tuple-element.7.features_ref, ...), custom_call_target="tpu_custom_call" | custom-call | tf_op jit(solution)/shard_map/pair_sketches/pallas_call | solution.py:371
  76.2 76.5 %scatter_sums.1 = f32[16,64,128]{2,1,0:T(8,128)S(1)} custom-call(f32[256,64,128]{2,1,0:T(8,128)S(1)} %get-tuple-element.11.x_ref), custom_call_target="tpu_custom_call" | custom-call | tf_op jit(solution)/shard_map/scatter_sums/pallas_call | solution.py:684
  152.8 0.8 copy.14
  (1 shorter events, 0.0 us)
Async XLA Ops:
  4.7 1.0 copy-start.1
  61.0 3.6 %copy-start = (f32[256,72,128]{2,1,0:T(8,128)}, f32[256,72,128]{2,1,0:T(8,128)S(1)}, u32[]{:S(2)}) copy-start(f32[256,72,128]{2,1,0:T(8,128)S(1)} %get-tuple-element.9.column_ref) | copy-start | bytes 28311556
  64.6 0.7 copy-start.2

commit v5 on v4

--- a/solution.py
+++ b/solution.py
@@ -464,20 +464,27 @@
     down = index_of(place - 1, side, core)
     up = index_of(place + 1, side, core)
 
-    def pass_on(q, half, here, forward, target):
+    def pass_on(z, half, here, forward, target):
+        q = index_of(z, side, core)
+
         @pl.when(here)
         def _():
             arrived(q, half)
 
         send(here & forward, q, half, target)
-        send(here, q, half, across)
+        send(here & (z > 0) & (z < line - 1) if half else here, q, half, across)
         send(here, q, half, sibling)
 
-    def relay(q, half, here):
+    def relay(z, half, here):
+        q = index_of(z, 1 - side, core)
+
         @pl.when(here)
         def _():
             arrived(q, half)
 
+        if half:
+            send(here & (z == 0) & (place < line - 1), q, half, up)
+            send(here & (z == line - 1) & (place > 0), q, half, down)
         send(here, q, half, sibling)
 
     for half in range(2):
@@ -497,17 +504,13 @@
     for step in range(1, line + 1):
         for half in range(2):
             if step < line:
-                pass_on(
-                    index_of(place - step, side, core), half, place >= step, place < line - 1, up
-                )
-                pass_on(
-                    index_of(place + step, side, core), half, place + step < line, place > 0, down
-                )
+                pass_on(place - step, half, place >= step, place < line - 1, up)
+                pass_on(place + step, half, place + step < line, place > 0, down)
             if step == 1:
-                relay(across, half, always)
+                relay(place, half, always)
             else:
-                relay(index_of(place - step + 1, 1 - side, core), half, place >= step - 1)
-                relay(index_of(place + step - 1, 1 - side, core), half, place + step - 1 < line)
+                relay(place - step + 1, half, place >= step - 1)
+                relay(place + step - 1, half, place + step - 1 < line)
     for z in range(line):
         for s in range(2):
             for half in range(2):
@@ -525,7 +528,7 @@
     line = owners // 4
     cl_dev, width, panels = left_sketch.shape
     shape = (owners * packed.shape[0],) + packed.shape[1:]
-    most = 2 * (4 + 3 * 2 * (line - 1) + 1 + 2 * (line - 1))
+    most = 2 * (4 + 3 * 2 * (line - 1)) + 4 * (1 + 2 * (line - 1))
     return pl.pallas_call(
         functools.partial(gather_kernel, line),
         out_shape=(
@@ -556,12 +559,14 @@
     side_buf,
     low_buf,
     high_buf,
+    edge_buf,
     send_sem,
     own_sem,
     core_sem,
     side_sem,
     low_sem,
     high_sem,
+    edge_sem,
 ):
     me, core, side, place = neighbours(line)
     size = out_ref.shape[0]
@@ -581,13 +586,28 @@
             device_id={"clus": index_of(place, side, 1 - core)},
         )
 
-    def to_side(z, index):
+    part = size // 2
+
+    def to_side(z, half, index):
+        rows = pl.ds(half * part, part)
         return pltpu.make_async_remote_copy(
-            src_ref=core_buf.at[z * 2 + 1 - side],
-            dst_ref=side_buf.at[z],
+            src_ref=core_buf.at[z * 2 + 1 - side, rows],
+            dst_ref=side_buf.at[z, rows],
             send_sem=send_sem.at[index],
-            recv_sem=side_sem.at[z],
+            recv_sem=side_sem.at[z * 2 + half],
             device_id={"clus": index_of(place, 1 - side, core)},
+        )
+
+    def crosses(z):
+        return (z > 0) & (z < line - 1)
+
+    def to_edge(end, index):
+        return pltpu.make_async_remote_copy(
+            src_ref=core_buf.at[end * 2 + 1 - side, pl.ds(part, part)],
+            dst_ref=edge_buf.at[min(end, 1)],
+            send_sem=send_sem.at[index],
+            recv_sem=edge_sem.at[min(end, 1)],
+            device_id={"clus": index_of(place + (1 if end else -1), side, core)},
         )
 
     def along(z, index, buf, sem, target):
@@ -622,14 +642,47 @@
         fetch(z, s).wait()
         to_sibling(z, s, 2 * k).wait_recv()
         core_buf[z * 2 + s] = core_buf[z * 2 + s] + own_buf[z * 2 + s]
-        to_side(z, 8 + k).start()
+        to_side(z, 0, 8 + k).start()
+
+        @pl.when(crosses(z))
+        def _(z=z, k=k):
+            to_side(z, 1, 15 + k).start()
+
+    for e, end in enumerate((0, line - 1)):
+        far = line - 1 - end
+
+        @pl.when(place != far)
+        def _(end=end, e=e):
+            to_edge(end, 0).wait_recv()
+            rows = pl.ds(part, part)
+            core_buf[end * 2 + 1 - side, rows] = core_buf[end * 2 + 1 - side, rows] + edge_buf[e]
+
+        @pl.when(place != end)
+        def _(end=end, e=e):
+            to_edge(end, 19 + e).start()
+
+        @pl.when(place == end)
+        def _(end=end, e=e):
+            to_side(end, 1, 21 + e).start()
+
     for k, z in enumerate(order):
         fetch(z, side).wait()
         to_sibling(z, side, 2 * k + 1).wait_recv()
         core_buf[z * 2 + side] = core_buf[z * 2 + side] + own_buf[z * 2 + side]
     for k, z in enumerate(order):
-        to_side(z, 8 + k).wait_recv()
-        side_buf[z] = side_buf[z] + core_buf[z * 2 + side]
+        first, second = pl.ds(0, part), pl.ds(part, part)
+        to_side(z, 0, 0).wait_recv()
+        side_buf[z, first] = side_buf[z, first] + core_buf[z * 2 + side, first]
+
+        @pl.when(crosses(z) | (z == place))
+        def _(z=z, second=second):
+            to_side(z, 1, 0).wait_recv()
+            side_buf[z, second] = side_buf[z, second] + core_buf[z * 2 + side, second]
+
+        @pl.when(jnp.logical_not(crosses(z) | (z == place)))
+        def _(z=z, second=second):
+            side_buf[z, second] = core_buf[z * 2 + side, second]
+
         if k < line - 1:
 
             @pl.when((z > place) & (place > 0))
@@ -665,7 +718,12 @@
     for k, z in enumerate(order):
         for j, s in enumerate((1 - side, side)):
             to_sibling(z, s, 2 * k + j).wait_send()
-        to_side(z, 8 + k).wait_send()
+        to_side(z, 0, 8 + k).wait_send()
+
+        @pl.when(crosses(z))
+        def _(z=z, k=k):
+            to_side(z, 1, 15 + k).wait_send()
+
         if k < line - 1:
 
             @pl.when(z > place)
@@ -675,6 +733,16 @@
             @pl.when(z < place)
             def _(z=z, k=k):
                 downward(z, 12 + k).wait_send()
+
+    for e, end in enumerate((0, line - 1)):
+
+        @pl.when(place != end)
+        def _(end=end, e=e):
+            to_edge(end, 19 + e).wait_send()
+
+        @pl.when(place == end)
+        def _(end=end, e=e):
+            to_side(end, 1, 21 + e).wait_send()
 
 
 def scatter_sums(outgoing, owners):
@@ -692,12 +760,14 @@
             pltpu.VMEM((line,) + block, jnp.float32),
             pltpu.VMEM((line,) + block, jnp.float32),
             pltpu.VMEM((line,) + block, jnp.float32),
-            pltpu.SemaphoreType.DMA((4 * line,)),
+            pltpu.VMEM((2, block[0] // 2) + block[1:], jnp.float32),
+            pltpu.SemaphoreType.DMA((23,)),
+            pltpu.SemaphoreType.DMA((2 * line,)),
             pltpu.SemaphoreType.DMA((2 * line,)),
             pltpu.SemaphoreType.DMA((2 * line,)),
             pltpu.SemaphoreType.DMA((line,)),
             pltpu.SemaphoreType.DMA((line,)),
-            pltpu.SemaphoreType.DMA((line,)),
+            pltpu.SemaphoreType.DMA((2,)),
         ],
         compiler_params=pltpu.CompilerParams(
             collective_id=1, has_side_effects=True, vmem_limit_bytes=vmem_budget

time: 155 us -> 174 us (1.12)
  the two profiles are of different devices: /device:TPU:4 before, /device:TPU:0 now
where the time goes in v5:
time: 174 us
  Pallas kernels  163 us (94%)
  local copies, waits for them, and re-layouts  7.68 us (4%)
  other arithmetic  1.86 us (1%)
    pallas_call x1, Pallas kernels, scatter_sums(): pl.pallas_call(functools.partial(scatter_kernel, line), out_shape=jax.Sha...  80.5 us
    pallas_call x1, Pallas kernels, gather_clusters(): pl.pallas_call(functools.partial(gather_kernel, line), out_shape=(jax.Sha...  52.9 us
    pallas_call x1, Pallas kernels, sketch_pairs(): pl.pallas_call(pair_kernel, grid_spec=pltpu.PrefetchScalarGridSpec(num_sc...  30 us
    unnamed x9, local copies, waits for them, and re-layouts  7.6 us

profile of v5, /device:TPU:0, one launch (start us, length us, event | category | flops | bytes accessed | tf_op | source)
XLA Modules:
  0.0 174.3 jit_solution(6221987030026164355)
XLA Ops:
  1.3 0.7 fusion.1
  2.0 0.1 pad.3.clone
  2.1 0.8 copy.10
  2.8 0.8 copy.11
  3.6 1.2 maximum_maximum_fusion.x_ref
  4.7 0.0 copy-start.1
  4.7 1.0 copy-done.1
  5.8 52.9 %gather_clusters.1 = (f32[256,72,128]{2,1,0:T(8,128)S(1)}, bf16[16,256,96]{2,1,0:T(8,128)(2,1)S(1)}, bf16[16,128,256]{2,1,0:T(8,128)(2,1)S(1)}) custom-call(f32[16,72,128]{2,1,0:T(8,128)S(1)} %maximum_maximum_fusion.x_ref, f32[16,64,128]{2,1,0:T(8,128)S(1)} %copy-done.1), custom_call_target="tpu_custom_call" | custom-call | tf_op jit(solution)/shard_map/gather_clusters/pallas_call | solution.py:532
  58.7 0.0 copy-start
  58.7 3.6 %copy-done = f32[256,72,128]{2,1,0:T(8,128)} copy-done((f32[256,72,128]{2,1,0:T(8,128)}, f32[256,72,128]{2,1,0:T(8,128)S(1)}, u32[]{:S(2)}) %copy-start) | copy-done | bytes 9437208
  62.3 0.0 copy-start.2
  62.3 0.7 copy-done.2
  62.9 30.0 %pair_sketches.1 = (f32[16,64,128]{2,1,0:T(8,128)}, f32[256,64,128]{2,1,0:T(8,128)S(1)}) custom-call(s32[1]{0:T(128)S(6)} %copy.13.live_ref, s32[128]{0:T(128)S(1)} %copy-done.2, s32[128]{0:T(128)S(1)} %get-tuple-element.13.global_row_ref, s32[128]{0:T(128)S(1)} %get-tuple-element.12.col_ref, bf16[16,256,96]{2,1,0:T(8,128)(2,1)S(1)} %get-tuple-element.7.features_ref, ...), custom_call_target="tpu_custom_call" | custom-call | tf_op jit(solution)/shard_map/pair_sketches/pallas_call | solution.py:371
  93.0 80.5 %scatter_sums.1 = f32[16,64,128]{2,1,0:T(8,128)S(1)} custom-call(f32[256,64,128]{2,1,0:T(8,128)S(1)} %get-tuple-element.11.x_ref), custom_call_target="tpu_custom_call" | custom-call | tf_op jit(solution)/shard_map/scatter_sums/pallas_call | solution.py:752
  173.5 0.8 copy.14
  (1 shorter events, 0.0 us)
Async XLA Ops:
  4.7 1.0 copy-start.1
  58.7 3.6 %copy-start = (f32[256,72,128]{2,1,0:T(8,128)}, f32[256,72,128]{2,1,0:T(8,128)S(1)}, u32[]{:S(2)}) copy-start(f32[256,72,128]{2,1,0:T(8,128)S(1)} %get-tuple-element.9.column_ref) | copy-start | bytes 28311556
  62.3 0.7 copy-start.2

commit v6 on v4

--- a/solution.py
+++ b/solution.py
@@ -464,20 +464,27 @@
     down = index_of(place - 1, side, core)
     up = index_of(place + 1, side, core)
 
-    def pass_on(q, half, here, forward, target):
+    def pass_on(z, half, here, forward, target):
+        q = index_of(z, side, core)
+
         @pl.when(here)
         def _():
             arrived(q, half)
 
         send(here & forward, q, half, target)
-        send(here, q, half, across)
+        send(here & (z > 0) & (z < line - 1) if half else here, q, half, across)
         send(here, q, half, sibling)
 
-    def relay(q, half, here):
+    def relay(z, half, here):
+        q = index_of(z, 1 - side, core)
+
         @pl.when(here)
         def _():
             arrived(q, half)
 
+        if half:
+            send(here & (z == 0) & (place < line - 1), q, half, up)
+            send(here & (z == line - 1) & (place > 0), q, half, down)
         send(here, q, half, sibling)
 
     for half in range(2):
@@ -497,17 +504,13 @@
     for step in range(1, line + 1):
         for half in range(2):
             if step < line:
-                pass_on(
-                    index_of(place - step, side, core), half, place >= step, place < line - 1, up
-                )
-                pass_on(
-                    index_of(place + step, side, core), half, place + step < line, place > 0, down
-                )
+                pass_on(place - step, half, place >= step, place < line - 1, up)
+                pass_on(place + step, half, place + step < line, place > 0, down)
             if step == 1:
-                relay(across, half, always)
+                relay(place, half, always)
             else:
-                relay(index_of(place - step + 1, 1 - side, core), half, place >= step - 1)
-                relay(index_of(place + step - 1, 1 - side, core), half, place + step - 1 < line)
+                relay(place - step + 1, half, place >= step - 1)
+                relay(place + step - 1, half, place + step - 1 < line)
     for z in range(line):
         for s in range(2):
             for half in range(2):
@@ -525,7 +528,7 @@
     line = owners // 4
     cl_dev, width, panels = left_sketch.shape
     shape = (owners * packed.shape[0],) + packed.shape[1:]
-    most = 2 * (4 + 3 * 2 * (line - 1) + 1 + 2 * (line - 1))
+    most = 2 * (4 + 3 * 2 * (line - 1)) + 4 * (1 + 2 * (line - 1))
     return pl.pallas_call(
         functools.partial(gather_kernel, line),
         out_shape=(

time: 155 us -> 147 us (0.948)
  the two profiles are of different devices: /device:TPU:4 before, /device:TPU:0 now
where the time goes in v6:
time: 147 us
  Pallas kernels  136 us (93%)
  local copies, waits for them, and re-layouts  7.68 us (5%)
  other arithmetic  1.86 us (1%)
    pallas_call x1, Pallas kernels, scatter_sums(): pl.pallas_call(functools.partial(scatter_kernel, line), out_shape=jax.Sha...  73.8 us
    pallas_call x1, Pallas kernels, gather_clusters(): pl.pallas_call(functools.partial(gather_kernel, line), out_shape=(jax.Sha...  52.9 us
    pallas_call x1, Pallas kernels, sketch_pairs(): pl.pallas_call(pair_kernel, grid_spec=pltpu.PrefetchScalarGridSpec(num_sc...  9.48 us
    unnamed x9, local copies, waits for them, and re-layouts  7.6 us

profile of v6, /device:TPU:0, one launch (start us, length us, event | category | flops | bytes accessed | tf_op | source)
XLA Modules:
  0.0 147.1 jit_solution(11840042621392978711)
XLA Ops:
  1.3 0.7 fusion.1
  2.0 0.1 pad.3.clone
  2.1 0.8 copy.10
  2.8 0.8 copy.11
  3.6 1.2 maximum_maximum_fusion.x_ref
  4.7 0.0 copy-start.1
  4.7 1.0 copy-done.1
  5.8 52.9 %gather_clusters.1 = (f32[256,72,128]{2,1,0:T(8,128)S(1)}, bf16[16,256,96]{2,1,0:T(8,128)(2,1)S(1)}, bf16[16,128,256]{2,1,0:T(8,128)(2,1)S(1)}) custom-call(f32[16,72,128]{2,1,0:T(8,128)S(1)} %maximum_maximum_fusion.x_ref, f32[16,64,128]{2,1,0:T(8,128)S(1)} %copy-done.1), custom_call_target="tpu_custom_call" | custom-call | tf_op jit(solution)/shard_map/gather_clusters/pallas_call | solution.py:532
  58.7 0.0 copy-start
  58.7 3.6 %copy-done = f32[256,72,128]{2,1,0:T(8,128)} copy-done((f32[256,72,128]{2,1,0:T(8,128)}, f32[256,72,128]{2,1,0:T(8,128)S(1)}, u32[]{:S(2)}) %copy-start) | copy-done | bytes 9437208
  62.3 0.0 copy-start.2
  62.3 0.7 copy-done.2
  62.9 9.5 %pair_sketches.1 = (f32[16,64,128]{2,1,0:T(8,128)}, f32[256,64,128]{2,1,0:T(8,128)S(1)}) custom-call(s32[1]{0:T(128)S(6)} %copy.13.live_ref, s32[128]{0:T(128)S(1)} %copy-done.2, s32[128]{0:T(128)S(1)} %get-tuple-element.13.global_row_ref, s32[128]{0:T(128)S(1)} %get-tuple-element.12.col_ref, bf16[16,256,96]{2,1,0:T(8,128)(2,1)S(1)} %get-tuple-element.7.features_ref, ...), custom_call_target="tpu_custom_call" | custom-call | tf_op jit(solution)/shard_map/pair_sketches/pallas_call | solution.py:371
  72.4 73.8 %scatter_sums.1 = f32[16,64,128]{2,1,0:T(8,128)S(1)} custom-call(f32[256,64,128]{2,1,0:T(8,128)S(1)} %get-tuple-element.11.x_ref), custom_call_target="tpu_custom_call" | custom-call | tf_op jit(solution)/shard_map/scatter_sums/pallas_call | solution.py:687
  146.3 0.8 copy.14
  (1 shorter events, 0.0 us)
Async XLA Ops:
  4.7 1.0 copy-start.1
  58.7 3.6 %copy-start = (f32[256,72,128]{2,1,0:T(8,128)}, f32[256,72,128]{2,1,0:T(8,128)S(1)}, u32[]{:S(2)}) copy-start(f32[256,72,128]{2,1,0:T(8,128)S(1)} %get-tuple-element.9.column_ref) | copy-start | bytes 28311556
  62.3 0.7 copy-start.2
